TPU v7x, 512 devices: a whole 4x8x8 slice. The times are simulated.
512 devices in a mesh: runs: 64 (over y, x, core), cells: 8 (over z).
Axes of the slice: x: 4, y: 8, z: 8, core: 2. Of those that a mesh axis runs over, the one named last changes fastest.
Arguments:
- maps: bfloat16 [8192, 16384], P('runs', 'cells'), may hold values from -6 to 6
- run_inputs: bfloat16 [8, 8192], P(None, 'runs'), may hold values from 0 to 1
- basis: bfloat16 [16384, 256], P('cells'), may hold values from -0.375 to 0.375
- amplitude: float32 [8], replicated, may hold values from 0.02 to 0.045
- length: float32 [8, 8], replicated, may hold values from 0.27 to 0.33
- noise: float32 [8192], P('runs'), may hold values from 0.1 to 0.2
Outputs:
- product: bfloat16 [8192, 16384], P('runs', 'cells')
All inputs are finite; a program needn't handle non-finite values.
Results may differ from a plain program's by a relative error of at most 0.0064.
Values may be sent and summed in bfloat16 or wider, within the bound.
A program may use at most 64 MiB of HBM per device.

v0:
```python
import math

import jax
import jax.numpy as jnp
from jax import lax
from jax.sharding import PartitionSpec as P


def make_fold(local_inputs, amp_used, len_used, rank):
    inverse = 1.0 / len_used
    owned = amp_used.shape[0]
    num_in = local_inputs.shape[0]
    row_count = local_inputs.shape[1]
    rows_scaled = local_inputs.astype(jnp.float32)[None, :, :] * inverse[:, :, None]
    rows_half = 0.5 * jnp.sum(rows_scaled * rows_scaled, axis=1)

    def fold(total, piece, start):
        inputs_piece, proj_piece = piece
        width = inputs_piece.shape[1]
        block = math.gcd(width, 1024)
        count = width // block
        cols_scaled = inputs_piece.astype(jnp.float32)[None, :, :] * inverse[:, :, None]
        cols_half = 0.5 * jnp.sum(cols_scaled * cols_scaled, axis=1)
        scaled_blocks = cols_scaled.reshape(owned, num_in, count, block).transpose(2, 0, 1, 3)
        half_blocks = cols_half.reshape(owned, count, block).transpose(1, 0, 2)
        proj_blocks = proj_piece.reshape(owned, rank, count, block).transpose(2, 0, 1, 3)

        def step(accum, parts):
            scaled_now, half_now, proj_now = parts
            logit = jnp.einsum(
                "qdr,qdc->qrc", rows_scaled, scaled_now, precision=lax.Precision.HIGHEST
            )
            logit = logit - rows_half[:, :, None] - half_now[:, None, :]
            tile = (amp_used[:, None, None] * jnp.exp(jnp.minimum(logit, 0.0))).astype(jnp.bfloat16)
            values = jnp.einsum("qrc,qkc->rqk", tile, proj_now, preferred_element_type=jnp.float32)
            return (accum + values.reshape(row_count, owned * rank), None)

        result, unused = lax.scan(step, total, (scaled_blocks, half_blocks, proj_blocks))
        return result

    return fold


def shards(maps, run_inputs, basis, amplitude, length, noise):
    lat = amplitude.shape[0]
    rank = basis.shape[1] // lat
    row_count = maps.shape[0]
    partial_proj = lax.dot_general(
        basis, maps, (((0,), (1,)), ((), ())), preferred_element_type=jnp.float32
    )
    summed = lax.psum(partial_proj, "cells")
    projected = summed.astype(jnp.bfloat16)
    fold = make_fold(run_inputs, amplitude, length, rank)
    empty = jnp.zeros((row_count, lat * rank), jnp.float32)
    values = fold(
        empty,
        (
            lax.all_gather(run_inputs, "runs", axis=1, tiled=True),
            lax.all_gather(projected, "runs", axis=1, tiled=True),
        ),
        jnp.int32(0),
    )
    latent = values.astype(jnp.bfloat16)
    expand = lax.dot_general(
        latent, basis, (((1,), (1,)), ((), ())), preferred_element_type=jnp.float32
    )
    return (expand + noise[:, None] * maps.astype(jnp.float32)).astype(jnp.bfloat16)


def solution(mesh):
    in_specs = (P("runs", "cells"), P(None, "runs"), P("cells", None), P(), P(), P("runs"))
    out_specs = P("runs", "cells")
    return jax.shard_map(shards, mesh=mesh, in_specs=in_specs, out_specs=out_specs, check_vma=False)
```

profile of v0, /device:TPU:1, one launch (start us, length us, event | category | flops | bytes accessed | tf_op | source)
XLA Modules:
  0.0 230.1 jit_solution(4648881709465107752)
XLA Ops:
  6.5 0.0 copy-start
  6.5 0.0 all-gather.2.cloned.1.call-start
  6.5 1.2 copy-done
  7.8 1.5 fusion.14
  9.3 31.3 %all-reduce.1 = bf16[256,128]{1,0:T(8,128)(2,1)} all-reduce(f32[256,128]{1,0:T(8,128)S(1)} %fusion.14), channel_id=1, replica_groups=mesh['runs'=64,'cells'=8] {'cells'}, use_global_device_ids=true, to_apply=%region_1.0 | all-reduce | flops 32768 | bytes 196608 | tf_op jit(solution)/shard_map/psum | solution.py:51
  40.6 0.0 all-gather.2.cloned.1.call-update
  40.7 0.7 convert_element_type.23
  41.3 58.4 %all_gather.7 = bf16[8,8192]{1,0:T(8,128)(2,1)S(1)} all-gather(bf16[8,128]{1,0:T(8,128)(2,1)} %param.9), channel_id=1, replica_groups=mesh['runs'=64,'cells'=8] {'runs'}, dimensions={1}, use_global_device_ids=true | all-gather | bytes 133120 | tf_op jit(solution)/shard_map/all_gather | solution.py:58
  99.8 0.7 broadcast_divide_fusion
  100.5 0.1 multiply_reduce_fusion.1
  100.6 0.7 multiply_reduce_fusion
  101.3 1.7 broadcast_multiply_fusion
  103.0 24.3 %all-gather.2.cloned.1.call-done = bf16[256,8192]{1,0:T(8,128)(2,1)} async-done(((bf16[256,128]{1,0:T(8,128)(2,1)}), bf16[256,8192]{1,0:T(8,128)(2,1)}) %all-gather.2.cloned.1.call-update) | async-done | bytes 4194320 | tf_op jit(solution)/shard_map/all_gather | solution.py:59
  127.3 6.5 %copy.9 = bf16[32,8,8,1024]{3,2,1,0:T(8,128)(2,1)S(1)} copy(bf16[32,8,8,1024]{3,1,2,0:T(8,128)(2,1)} %bitcast.40) | data formatting | bytes 8388608
  133.8 0.0 copy-start.3
  133.8 4.3 %copy.11 = bf16[8,32,8,1024]{3,1,0,2:T(8,128)(2,1)} copy(bf16[8,32,8,1024]{3,2,1,0:T(8,128)(2,1)S(1)} %bitcast.38) | data formatting | bytes 8388608 | tf_op jit(solution)/shard_map/reshape | solution.py:26
  138.0 0.0 copy-done.3
  138.0 0.0 copy-start.1
  138.1 0.0 copy-start.2
  138.1 83.9 %while.11 = (s32[]{:T(128)}, f32[128,256]{0,1:T(8,128)S(1)}, bf16[8,8,32,1024]{3,2,1,0:T(8,128)(2,1)}, f32[8]{0:T(128)S(1)}, f32[8,8,8,1024]{3,2,1,0:T(8,128)}, ...) while((s32[]{:T(128)}, f32[128,256]{0,1:T(8,128)S(1)}, ...), condition=%wide.region_4.5_spmd.clone, body=%wide.region_3.4_spmd.clone.sunk | while | flops 173088768 | bytes 5611947 | solution.py:38
  138.1 9.0 %multiply_convert_fusion.2 = bf16[8,1024,128]{2,1,0:T(8,128)(2,1)S(1)} fusion(f32[8]{0:T(128)S(1)} %get-tuple-element.180, f32[8,1024]{1,0:T(8,128)S(1)} %dynamic-slice_bitcast_fusion.2, f32[8,128]{1,0:T(8,128)S(1)} %get-tuple-element.182, f32[8,8,8,1024]{3,2,1,0:T(8,128)} %get-tuple-element.181, s32[]{:T(128)S(6)} %copy.15, ...), kind=kOutput, calls=%fused_computation.1.clone.1 | convolution fusion | flops 105914368 | bytes 2400548 | tf_op jit(solution)/shard_map/while/body/eval_jaxpr/qdr,qdc->qrc/dot_general | solution.py:30
  147.0 1.5 fusion.28
  148.6 8.9 %multiply_convert_fusion.2 = bf16[8,1024,128]{2,1,0:T(8,128)(2,1)S(1)} fusion(f32[8]{0:T(128)S(1)} %get-tuple-element.180, f32[8,1024]{1,0:T(8,128)S(1)} %dynamic-slice_bitcast_fusion.2, f32[8,128]{1,0:T(8,128)S(1)} %get-tuple-element.182, f32[8,8,8,1024]{3,2,1,0:T(8,128)} %get-tuple-element.181, s32[]{:T(128)S(6)} %copy.15, ...), kind=kOutput, calls=%fused_computation.1.clone.1 | convolution fusion | flops 105914368 | bytes 2400548 | tf_op jit(solution)/shard_map/while/body/eval_jaxpr/qdr,qdc->qrc/dot_general | solution.py:30
  157.5 1.5 fusion.28
  159.1 8.9 %multiply_convert_fusion.2 = bf16[8,1024,128]{2,1,0:T(8,128)(2,1)S(1)} fusion(f32[8]{0:T(128)S(1)} %get-tuple-element.180, f32[8,1024]{1,0:T(8,128)S(1)} %dynamic-slice_bitcast_fusion.2, f32[8,128]{1,0:T(8,128)S(1)} %get-tuple-element.182, f32[8,8,8,1024]{3,2,1,0:T(8,128)} %get-tuple-element.181, s32[]{:T(128)S(6)} %copy.15, ...), kind=kOutput, calls=%fused_computation.1.clone.1 | convolution fusion | flops 105914368 | bytes 2400548 | tf_op jit(solution)/shard_map/while/body/eval_jaxpr/qdr,qdc->qrc/dot_general | solution.py:30
  168.0 1.5 fusion.28
  169.6 8.9 %multiply_convert_fusion.2 = bf16[8,1024,128]{2,1,0:T(8,128)(2,1)S(1)} fusion(f32[8]{0:T(128)S(1)} %get-tuple-element.180, f32[8,1024]{1,0:T(8,128)S(1)} %dynamic-slice_bitcast_fusion.2, f32[8,128]{1,0:T(8,128)S(1)} %get-tuple-element.182, f32[8,8,8,1024]{3,2,1,0:T(8,128)} %get-tuple-element.181, s32[]{:T(128)S(6)} %copy.15, ...), kind=kOutput, calls=%fused_computation.1.clone.1 | convolution fusion | flops 105914368 | bytes 2400548 | tf_op jit(solution)/shard_map/while/body/eval_jaxpr/qdr,qdc->qrc/dot_general | solution.py:30
  178.5 1.5 fusion.28
  180.0 8.9 %multiply_convert_fusion.2 = bf16[8,1024,128]{2,1,0:T(8,128)(2,1)S(1)} fusion(f32[8]{0:T(128)S(1)} %get-tuple-element.180, f32[8,1024]{1,0:T(8,128)S(1)} %dynamic-slice_bitcast_fusion.2, f32[8,128]{1,0:T(8,128)S(1)} %get-tuple-element.182, f32[8,8,8,1024]{3,2,1,0:T(8,128)} %get-tuple-element.181, s32[]{:T(128)S(6)} %copy.15, ...), kind=kOutput, calls=%fused_computation.1.clone.1 | convolution fusion | flops 105914368 | bytes 2400548 | tf_op jit(solution)/shard_map/while/body/eval_jaxpr/qdr,qdc->qrc/dot_general | solution.py:30
  188.9 1.5 fusion.28
  190.5 8.9 %multiply_convert_fusion.2 = bf16[8,1024,128]{2,1,0:T(8,128)(2,1)S(1)} fusion(f32[8]{0:T(128)S(1)} %get-tuple-element.180, f32[8,1024]{1,0:T(8,128)S(1)} %dynamic-slice_bitcast_fusion.2, f32[8,128]{1,0:T(8,128)S(1)} %get-tuple-element.182, f32[8,8,8,1024]{3,2,1,0:T(8,128)} %get-tuple-element.181, s32[]{:T(128)S(6)} %copy.15, ...), kind=kOutput, calls=%fused_computation.1.clone.1 | convolution fusion | flops 105914368 | bytes 2400548 | tf_op jit(solution)/shard_map/while/body/eval_jaxpr/qdr,qdc->qrc/dot_general | solution.py:30
  199.4 1.5 fusion.28
  201.0 8.9 %multiply_convert_fusion.2 = bf16[8,1024,128]{2,1,0:T(8,128)(2,1)S(1)} fusion(f32[8]{0:T(128)S(1)} %get-tuple-element.180, f32[8,1024]{1,0:T(8,128)S(1)} %dynamic-slice_bitcast_fusion.2, f32[8,128]{1,0:T(8,128)S(1)} %get-tuple-element.182, f32[8,8,8,1024]{3,2,1,0:T(8,128)} %get-tuple-element.181, s32[]{:T(128)S(6)} %copy.15, ...), kind=kOutput, calls=%fused_computation.1.clone.1 | convolution fusion | flops 105914368 | bytes 2400548 | tf_op jit(solution)/shard_map/while/body/eval_jaxpr/qdr,qdc->qrc/dot_general | solution.py:30
  209.9 1.5 fusion.28
  211.5 8.9 %multiply_convert_fusion.2 = bf16[8,1024,128]{2,1,0:T(8,128)(2,1)S(1)} fusion(f32[8]{0:T(128)S(1)} %get-tuple-element.180, f32[8,1024]{1,0:T(8,128)S(1)} %dynamic-slice_bitcast_fusion.2, f32[8,128]{1,0:T(8,128)S(1)} %get-tuple-element.182, f32[8,8,8,1024]{3,2,1,0:T(8,128)} %get-tuple-element.181, s32[]{:T(128)S(6)} %copy.15, ...), kind=kOutput, calls=%fused_computation.1.clone.1 | convolution fusion | flops 105914368 | bytes 2400548 | tf_op jit(solution)/shard_map/while/body/eval_jaxpr/qdr,qdc->qrc/dot_general | solution.py:30
  220.4 1.5 fusion.28
  221.9 0.0 copy-done.1
  221.9 0.0 copy-done.2
  222.0 1.3 fusion.12
  (20 shorter events, 0.3 us)
Async XLA Ops:
  6.5 1.2 copy-start
  6.5 120.7 %all-gather.2.cloned.1.call-start = ((), (), s32[]{:S(2)}) async-start(), calls=%async_computation | async-start | bytes 4259840 | tf_op jit(solution)/shard_map/all_gather | solution.py:59
  133.8 4.3 %copy-start.3 = (f32[8]{0:T(128)S(1)}, f32[8]{0:T(128)}, u32[]{:S(2)}) copy-start(f32[8]{0:T(128)} %param.11) | copy-start | bytes 100
  138.0 83.9 %copy-start.1 = (bf16[128,2048]{1,0:T(8,128)(2,1)S(1)}, bf16[128,2048]{1,0:T(8,128)(2,1)}, u32[]{:S(2)}) copy-start(bf16[128,2048]{1,0:T(8,128)(2,1)} %param.8) | copy-start | bytes 1572868
  138.1 83.9 %copy-start.2 = (f32[128]{0:T(128)S(1)}, f32[128]{0:T(128)}, u32[]{:S(2)}) copy-start(f32[128]{0:T(128)} %param.13) | copy-start | bytes 1540
Sparse Core Ops, SparseCore 0:
  40.8 86.4 all-gather.1
where the time goes:
time: 231 us; the launch traced here: 230 us
  blocking collectives  89.7 us (39%)
  matrix products  86 us (37%)
  waiting for transfers between devices  24.3 us (11%)
  between operations  13.5 us (6%)
  local copies, waits for them, and re-layouts  12.1 us (5%)
  other arithmetic  4.09 us (2%)
    dot_general x8, matrix products, step(): jnp.einsum('qdr,qdc->qrc', rows_scaled, scaled_now, precision=lax.Precisi...  71.3 us
    all_gather x1, blocking collectives, shards(): lax.all_gather(run_inputs, 'runs', axis=1, tiled=True)  58.4 us
    psum x1, blocking collectives, shards(): summed = lax.psum(partial_proj, 'cells')  31.3 us
    all_gather x1, waiting for transfers between devices, shards(): lax.all_gather(projected, 'runs', axis=1, tiled=True)  24.3 us
    dot_general x8, matrix products, step(): jnp.einsum('qrc,qkc->rqk', tile, proj_now, preferred_element_type=jnp.flo...  11.9 us
    unnamed x9, local copies, waits for them, and re-layouts  7.75 us
  transfers between devices with their start and end apart: 1, of which 1 were waited for; matrix products, arithmetic and copies ran while one was open for 2% of the time, Pallas kernels for 0%

commit v1 on v0

v1 whole, which is shorter than its diff:
```python
import jax
import jax.numpy as jnp
from jax import lax
from jax.experimental import pallas as pl
from jax.experimental.pallas import tpu as pltpu
from jax.sharding import PartitionSpec as P

MESH = pl.DeviceIdType.MESH
F32 = jnp.float32
BF16 = jnp.bfloat16
NY, NX, NC, NZ = 8, 4, 2, 8
NJ = NX * NC
ROWS = 128
RANK = 32
DIN = 8
CELLS = 2048
WIDTH = NZ * RANK
LOADS = 4
STEP = CELLS // LOADS


def split3(value):
    high = value.astype(BF16).astype(F32)
    rest = value - high
    mid = rest.astype(BF16).astype(F32)
    return high, mid, rest - mid


def pick(index, *values):
    out = jnp.zeros((8, ROWS), F32)
    for place, value in enumerate(values):
        out = jnp.where(index == place, value, out)
    return out


def kernel(
    x_ref, amp_ref, len_ref, noise_ref, maps_hbm, basis_hbm, out_hbm,
    maps, basis, outs, rows_x, cols_x, part_wide, part, part_in, proj, tile, side,
    sums, sums_in, latent, load_sem, store_sem, send_sem, recv_sem,
):
    run = lax.axis_index("runs")
    z = lax.axis_index("cells")
    y, j = run // NJ, run % NJ
    x, core = j // NC, j % NC

    def along_z(step):
        return (run, (z + step + NZ) % NZ)

    def along_y(step):
        return (((y + step + NY) % NY) * NJ + j, z)

    def along_j(slot, sign=1):
        dx, dc = slot // NC, slot % NC
        return (y * NJ + ((x + sign * dx + NX) % NX) * NC + (core + dc) % NC, z)

    barrier = pltpu.get_barrier_semaphore()
    for step in range(1, 8):
        for device in (along_z(step), along_y(step), along_j(step)):
            pl.semaphore_signal(barrier, inc=1, device_id=device, device_id_type=MESH)

    loads = []
    for c in range(LOADS):
        now = pl.ds(c * STEP, STEP)
        loads.append((
            pltpu.make_async_copy(maps_hbm.at[:, now], maps.at[:, now], load_sem.at[0, c]),
            pltpu.make_async_copy(basis_hbm.at[now], basis.at[now], load_sem.at[1, c]),
        ))
        for load in loads[-1]:
            load.start()

    def remote(phase, slot, source, target, device):
        return pltpu.make_async_remote_copy(
            src_ref=source, dst_ref=target, send_sem=send_sem.at[phase, slot],
            recv_sem=recv_sem.at[phase, slot], device_id=device, device_id_type=MESH,
        )

    mine = x_ref[...].astype(F32)
    rows_x[0] = mine
    cols_x[0] = mine
    pl.semaphore_wait(barrier, 21)

    sent = []
    rows_in = {}
    cols_in = {}
    for slot in range(1, 8):
        rows_in[slot] = remote(0, slot, rows_x.at[0], rows_x.at[slot], along_y(slot))
        cols_in[slot] = remote(1, slot, cols_x.at[0], cols_x.at[slot], along_j(slot))
        rows_in[slot].start()
        cols_in[slot].start()

    total = jnp.zeros((ROWS, WIDTH), F32)
    for c in range(LOADS):
        for load in loads[c]:
            load.wait()
        now = pl.ds(c * STEP, STEP)
        total = total + jnp.dot(maps[:, now], basis[now, :], preferred_element_type=F32)
    turned = total.T.reshape(NZ, RANK, ROWS)
    part_wide[...] = turned
    part[...] = turned.astype(BF16)
    part_sends = {}
    for slot in (4, 3, 5, 2, 6, 1, 7):
        peer = along_z(slot)
        part_sends[slot] = remote(2, slot, part.at[peer[1]], part_in.at[slot], peer)
        part_sends[slot].start()

    index = lax.broadcasted_iota(jnp.int32, (8, ROWS), 0)
    length = len_ref[pl.ds(z, 1), :]
    square = (DIN, DIN)
    eye = lax.broadcasted_iota(jnp.int32, square, 0) == lax.broadcasted_iota(jnp.int32, square, 1)
    column = jnp.sum(jnp.where(eye, jnp.broadcast_to(length, square), 0.0), axis=1, keepdims=True)
    inverse = 1.0 / column
    squared = inverse * inverse
    amp = amp_ref[z]

    def halves(inputs):
        scaled = inputs * inverse
        return split3(0.5 * jnp.sum(scaled * scaled, axis=0, keepdims=True))

    for slot in range(1, 8):
        rows_in[slot].wait_recv()
    for slot in range(NY):
        inputs = rows_x[slot]
        ha, hb, hc = halves(inputs)
        wa, wb, wc = split3(inputs * squared)
        tail = pick(index, -ha, -hb, -hc, -1.0, -1.0, -1.0)
        side[:, slot * ROWS:(slot + 1) * ROWS] = jnp.concatenate([wa, wb, wc, tail], 0).astype(BF16)
    for slot in range(1, 8):
        cols_in[slot].wait_recv()

    @pl.loop(0, NJ)
    def _(slot):
        inputs = cols_x[slot]
        ha, hb, hc = halves(inputs)
        tail = pick(index, 1.0, 1.0, 1.0, ha, hb, hc)
        left = jnp.concatenate([inputs, inputs, inputs, tail], 0).T.astype(BF16)
        logit = jnp.dot(left, side[...], preferred_element_type=F32)
        tile[slot] = (amp * jnp.exp(jnp.minimum(logit, 0.0))).astype(BF16)

    own = part_wide[z]
    for slot in range(1, 8):
        part_sends[slot].wait_recv()
        own = own + part_in[slot].astype(F32)
    proj[0] = own.astype(BF16)
    proj_sends = {}
    for slot in (4, 5, 2, 3, 6, 7, 1):
        proj_sends[slot] = remote(3, slot, proj.at[0], proj.at[slot], along_j(slot))
        proj_sends[slot].start()

    values = jnp.zeros((RANK, NY * ROWS), F32)
    for pair in (0, 1, 3, 2):
        for slot in (2 * pair, 2 * pair + 1):
            if slot:
                proj_sends[slot].wait_recv()
        block = jnp.concatenate([proj[2 * pair], proj[2 * pair + 1]], 1)
        weights = tile[2 * pair:2 * pair + 2].reshape(2 * ROWS, NY * ROWS)
        values = values + jnp.dot(block, weights, preferred_element_type=F32)

    sum_sends = {}
    for slot in (4, 3, 5, 2, 6, 1, 7):
        sums[slot] = values[:, slot * ROWS:(slot + 1) * ROWS].astype(BF16)
        sum_sends[slot] = remote(4, slot, sums.at[slot], sums_in.at[slot], along_y(-slot))
        sum_sends[slot].start()
    final = values[:, :ROWS]
    for slot in range(1, 8):
        sum_sends[slot].wait_recv()
        final = final + sums_in[slot].astype(F32)
    latent[z] = final.astype(BF16)
    latent_sends = {}
    for slot in (4, 3, 5, 2, 6, 1, 7):
        latent_sends[slot] = remote(5, slot, latent.at[z], latent.at[z], along_z(slot))
        latent_sends[slot].start()

    whole = (ROWS, ROWS)
    eye = lax.broadcasted_iota(jnp.int32, whole, 0) == lax.broadcasted_iota(jnp.int32, whole, 1)
    spread = jnp.where(eye, jnp.broadcast_to(noise_ref[...], whole), 0.0)
    noise = jnp.sum(spread, axis=1, keepdims=True)

    for slot in range(1, 8):
        latent_sends[slot].wait_recv()
    mixed = latent[...].reshape(WIDTH, ROWS).astype(F32).T.astype(BF16)
    stores = []
    for c in range(LOADS):
        now = pl.ds(c * STEP, STEP)
        expand = lax.dot_general(
            mixed, basis[now, :], (((1,), (1,)), ((), ())), preferred_element_type=F32
        )
        outs[:, now] = (expand + noise * maps[:, now].astype(F32)).astype(BF16)
        stores.append(pltpu.make_async_copy(outs.at[:, now], out_hbm.at[:, now], store_sem.at[c]))
        stores[-1].start()

    for group in (rows_in, cols_in, part_sends, proj_sends, sum_sends, latent_sends):
        for slot in range(1, 8):
            group[slot].wait_send()
    for store in stores:
        store.wait()


def shards(maps, run_inputs, basis, amplitude, length, noise):
    vmem = pl.BlockSpec(memory_space=pltpu.VMEM)
    smem = pl.BlockSpec(memory_space=pltpu.SMEM)
    hbm = pl.BlockSpec(memory_space=pl.ANY)
    block = (8, RANK, ROWS)
    return pl.pallas_call(
        kernel,
        out_shape=jax.ShapeDtypeStruct((ROWS, CELLS), BF16),
        in_specs=[vmem, smem, vmem, vmem, hbm, hbm],
        out_specs=hbm,
        scratch_shapes=[
            pltpu.VMEM((ROWS, CELLS), BF16),
            pltpu.VMEM((CELLS, WIDTH), BF16),
            pltpu.VMEM((ROWS, CELLS), BF16),
            pltpu.VMEM((NY, DIN, ROWS), F32),
            pltpu.VMEM((NJ, DIN, ROWS), F32),
            pltpu.VMEM(block, F32),
            pltpu.VMEM(block, BF16),
            pltpu.VMEM(block, BF16),
            pltpu.VMEM(block, BF16),
            pltpu.VMEM((NJ, ROWS, NY * ROWS), BF16),
            pltpu.VMEM((RANK, NY * ROWS), BF16),
            pltpu.VMEM(block, BF16),
            pltpu.VMEM(block, BF16),
            pltpu.VMEM(block, BF16),
            pltpu.SemaphoreType.DMA((2, LOADS)),
            pltpu.SemaphoreType.DMA((LOADS,)),
            pltpu.SemaphoreType.DMA((6, 8)),
            pltpu.SemaphoreType.DMA((6, 8)),
        ],
        compiler_params=pltpu.CompilerParams(
            collective_id=0, has_side_effects=True, vmem_limit_bytes=32 * 1024 * 1024
        ),
    )(run_inputs, amplitude, length, noise.reshape(1, ROWS), maps, basis)


def solution(mesh):
    in_specs = (P("runs", "cells"), P(None, "runs"), P("cells", None), P(), P(), P("runs"))
    out_specs = P("runs", "cells")
    return jax.shard_map(shards, mesh=mesh, in_specs=in_specs, out_specs=out_specs, check_vma=False)
```

time: 231 us -> 42.3 us (0.18)
  blocking collectives: 89.7 us -> 0 us
  matrix products: 86 us -> 0 us
  Pallas kernels: 0 us -> 36.9 us
  waiting for transfers between devices: 24.3 us -> 0 us
  between operations: 13.5 us -> 0.02 us
  local copies, waits for them, and re-layouts: 12.1 us -> 5.1 us
  other arithmetic: 4.09 us -> 0 us
    dot_general x18 -> x0, matrix products: 86 us -> none  [the longest x8 71.3 us: step(): jnp.einsum('qdr,qdc->qrc', rows_scaled, scaled_now, precision=lax.Precisi...]
    all_gather x1 -> x0, blocking collectives: 58.4 us -> none  [shards(): lax.all_gather(run_inputs, 'runs', axis=1, tiled=True)]
    pallas_call x0 -> x1, Pallas kernels: none -> 36.9 us  [shards(): pl.pallas_call(kernel, out_shape=jax.ShapeDtypeStruct((ROWS, CELLS), BF16...]
    psum x1 -> x0, blocking collectives: 31.3 us -> none  [shards(): summed = lax.psum(partial_proj, 'cells')]
    all_gather x1 -> x0, waiting for transfers between devices: 24.3 us -> none  [shards(): lax.all_gather(projected, 'runs', axis=1, tiled=True)]
    reshape x1 -> x0, local copies, waits for them, and re-layouts: 4.25 us -> none  [fold(): proj_piece.reshape(owned, rank, count, block).transpose(2, 0, 1, 3)]
    unnamed x9 -> x13, local copies, waits for them, and re-layouts: 7.75 us -> 5.1 us
  transfers between devices with their start and end apart: 1 -> 0, of which waited for: 1 -> 0; matrix products, arithmetic and copies ran while one was open for 2% -> 0% of each run, Pallas kernels for 0% -> 0%
where the time goes in v1:
time: 42.3 us; the launch traced here: 42 us
  Pallas kernels  36.9 us (87%)
  local copies, waits for them, and re-layouts  5.1 us (12%)
    pallas_call x1, Pallas kernels, shards(): pl.pallas_call(kernel, out_shape=jax.ShapeDtypeStruct((ROWS, CELLS), BF16...  36.9 us
    unnamed x13, local copies, waits for them, and re-layouts  5.1 us

profile of v1, /device:TPU:1, one launch (start us, length us, event | category | flops | bytes accessed | tf_op | source)
XLA Modules:
  0.0 42.0 jit_solution(17346271901363987426)
XLA Ops:
  0.0 0.0 copy-start.5
  0.0 0.0 copy-start.4
  0.0 0.7 %copy-done.5 = f32[128]{0:T(128)S(1)} copy-done((f32[128]{0:T(128)S(1)}, f32[128]{0:T(128)}, u32[]{:S(2)}) %copy-start.5) | copy-done | bytes 536
  0.7 0.0 copy-done.4
  0.7 0.0 copy-start
  0.7 1.2 %copy-done = bf16[2048,256]{1,0:T(8,128)(2,1)S(1)} copy-done((bf16[2048,256]{1,0:T(8,128)(2,1)S(1)}, bf16[2048,256]{1,0:T(8,128)(2,1)}, u32[]{:S(2)}) %copy-start) | copy-done | bytes 1048600
  1.9 0.0 copy-start.1
  1.9 1.0 %copy-done.1 = bf16[128,2048]{1,0:T(8,128)(2,1)S(1)} copy-done((bf16[128,2048]{1,0:T(8,128)(2,1)S(1)}, bf16[128,2048]{1,0:T(8,128)(2,1)}, u32[]{:S(2)}) %copy-start.1) | copy-done | bytes 524312
  2.9 0.0 copy-start.2
  2.9 0.7 %copy-done.2 = f32[8,8]{1,0:T(8,128)S(1)} copy-done((f32[8,8]{1,0:T(8,128)S(1)}, f32[8,8]{1,0:T(8,128)}, u32[]{:S(2)}) %copy-start.2) | copy-done | bytes 280
  3.6 0.0 copy-start.3
  3.6 0.7 %copy-done.3 = bf16[8,128]{1,0:T(8,128)(2,1)S(1)} copy-done((bf16[8,128]{1,0:T(8,128)(2,1)S(1)}, bf16[8,128]{1,0:T(8,128)(2,1)}, u32[]{:S(2)}) %copy-start.3) | copy-done | bytes 2072
  4.3 36.9 %shard_map.64 = bf16[128,2048]{1,0:T(8,128)(2,1)S(1)} custom-call(bf16[8,128]{1,0:T(8,128)(2,1)S(1)} %copy-done.3, f32[8]{0:T(128)S(1)} %copy-done.4, f32[8,8]{1,0:T(8,128)S(1)} %copy-done.2, f32[1,128]{1,0:T(1,128)S(1)} %bitcast.1, bf16[128,2048]{1,0:T(8,128)(2,1)S(1)} %copy-done.1, bf16[2048,256]{1,0:T(8,128)(2,1)S(1)} %copy-done), custom_call_target="tpu_custom_call" | custom-call | tf_op jit(solution)/shard_map/pallas_call | solution.py:203
  41.2 0.8 %copy.8 = bf16[128,2048]{1,0:T(8,128)(2,1)} copy(bf16[128,2048]{1,0:T(8,128)(2,1)S(1)} %shard_map.64) | data formatting | bytes 1048576
Async XLA Ops:
  0.0 0.7 %copy-start.5 = (f32[128]{0:T(128)S(1)}, f32[128]{0:T(128)}, u32[]{:S(2)}) copy-start(f32[128]{0:T(128)} %param.11) | copy-start | bytes 1540
  0.0 0.7 %copy-start.4 = (f32[8]{0:T(128)S(1)}, f32[8]{0:T(128)}, u32[]{:S(2)}) copy-start(f32[8]{0:T(128)} %amp_ref.1) | copy-start | bytes 100
  0.7 1.2 %copy-start = (bf16[2048,256]{1,0:T(8,128)(2,1)S(1)}, bf16[2048,256]{1,0:T(8,128)(2,1)}, u32[]{:S(2)}) copy-start(bf16[2048,256]{1,0:T(8,128)(2,1)} %basis_hbm.1) | copy-start | bytes 3145732
  1.9 1.0 %copy-start.1 = (bf16[128,2048]{1,0:T(8,128)(2,1)S(1)}, bf16[128,2048]{1,0:T(8,128)(2,1)}, u32[]{:S(2)}) copy-start(bf16[128,2048]{1,0:T(8,128)(2,1)} %maps_hbm.1) | copy-start | bytes 1572868
  2.9 0.7 %copy-start.2 = (f32[8,8]{1,0:T(8,128)S(1)}, f32[8,8]{1,0:T(8,128)}, u32[]{:S(2)}) copy-start(f32[8,8]{1,0:T(8,128)} %len_ref.1) | copy-start | bytes 772
  3.6 0.7 %copy-start.3 = (bf16[8,128]{1,0:T(8,128)(2,1)S(1)}, bf16[8,128]{1,0:T(8,128)(2,1)}, u32[]{:S(2)}) copy-start(bf16[8,128]{1,0:T(8,128)(2,1)} %x_ref.1) | copy-start | bytes 6148

commit v2 on v0

v2 whole, which is shorter than its diff:
```python
import jax
import jax.numpy as jnp
from jax import lax
from jax.experimental import pallas as pl
from jax.experimental.pallas import tpu as pltpu
from jax.sharding import PartitionSpec as P

MESH = pl.DeviceIdType.MESH
F32 = jnp.float32
BF16 = jnp.bfloat16
NY, NX, NC, NZ = 8, 4, 2, 8
ROWS = 128
PAIR = NC * ROWS
RANK = 32
DIN = 8
CELLS = 2048
WIDTH = NZ * RANK
LOADS = 4
STEP = CELLS // LOADS
FAR = (4, 3, 5, 2, 6, 1, 7)
ROW, COL, PART, PROJ, SUM, LAT0, LAT1 = range(7)


def split3(value):
    high = value.astype(BF16).astype(F32)
    rest = value - high
    mid = rest.astype(BF16).astype(F32)
    return high, mid, rest - mid


def pick(index, *values):
    out = jnp.zeros(index.shape, F32)
    for place, value in enumerate(values):
        out = jnp.where(index == place, value, out)
    return out


def kernel(
    x_hbm, amp_hbm, len_hbm, noise_hbm, maps_hbm, basis_hbm, out_ref,
    x_ref, amp_ref, len_ref, noise_ref, maps, basis, basis_t, base, mine, rows_x, cols_x,
    part_wide, part, part_in, proj, left, side, tile, sums, sums_in, lat_src, latent,
    load_sem, send_sem, recv_sem,
):
    run = lax.axis_index("runs")
    z = lax.axis_index("cells")
    y, x, core = run // (NX * NC), (run // NC) % NX, run % NC
    owner = core == 1

    def at(dy, dx, to, dz):
        place = ((y + dy + NY) % NY) * (NX * NC) + ((x + dx + NX) % NX) * NC + to
        return (place, (z + dz + NZ) % NZ)

    loads = []
    for c in range(LOADS):
        now = pl.ds(c * STEP, STEP)
        loads.append((
            pltpu.make_async_copy(maps_hbm.at[:, now], maps.at[:, now], load_sem.at[0, c]),
            pltpu.make_async_copy(basis_hbm.at[now], basis.at[now], load_sem.at[1, c]),
        ))
    small = [
        pltpu.make_async_copy(source, target, load_sem.at[2, place])
        for place, (source, target) in enumerate(
            ((x_hbm, x_ref), (len_hbm, len_ref), (amp_hbm, amp_ref), (noise_hbm, noise_ref))
        )
    ]
    for load in (*small, *loads[0], *loads[1], *loads[2], *loads[3]):
        load.start()

    barrier = pltpu.get_barrier_semaphore()

    def greet(device):
        pl.semaphore_signal(barrier, inc=1, device_id=device, device_id_type=MESH)

    @pl.when(owner)
    def _():
        for d in FAR:
            for to in range(NC):
                greet(at(d, 0, to, 0))
                greet(at(0, 0, to, d))
        for d in (2, 1, 3):
            for to in range(NC):
                greet(at(0, d, to, 0))
        greet(at(0, 0, 0, 0))

    @pl.when(jnp.logical_not(owner))
    def _():
        for d in (*FAR, 0):
            greet(at(0, 0, 1, d))

    def remote(phase, slot, source, target, device, to=0):
        return pltpu.make_async_remote_copy(
            src_ref=source, dst_ref=target, send_sem=send_sem.at[phase, slot],
            recv_sem=recv_sem.at[phase, slot, to], device_id=device, device_id_type=MESH,
        )

    def send_row(d):
        return remote(ROW, d, mine, rows_x.at[d, core], at(d, 0, 1, 0), core)

    def send_col(d):
        return remote(COL, d, mine, cols_x.at[d, core], at(0, d, 1, 0), core)

    def send_part(d):
        return remote(PART, d, part.at[(z + d) % NZ], part_in.at[d, core], at(0, 0, 1, d), core)

    def send_proj(d):
        return remote(PROJ, d, proj.at[0], proj.at[d], at(0, d, 1, 0))

    def send_sum(d):
        return remote(SUM, d, sums.at[d], sums_in.at[d], at(-d, 0, 1, 0))

    def send_latent(d, to):
        return remote(LAT0 + to, d, lat_src.at[to], latent.at[z], at(0, 0, to, d))

    def got(phase, slot, to, target):
        pltpu.make_async_remote_copy(
            src_ref=target, dst_ref=target, send_sem=send_sem.at[phase, slot],
            recv_sem=recv_sem.at[phase, slot, to], device_id=at(0, 0, 1, 1), device_id_type=MESH,
        ).wait_recv()

    for load in small:
        load.wait()
    mine[...] = x_ref[...].astype(F32)

    @pl.when(owner)
    def _():
        pl.semaphore_wait(barrier, 25)
        rows_x[0, 1] = mine[...]

    @pl.when(jnp.logical_not(owner))
    def _():
        pl.semaphore_wait(barrier, 18)
        send_row(0).start()

    for d in FAR:
        send_row(d).start()
    for d in (2, 1, 3):
        send_col(d).start()

    total = jnp.zeros((ROWS, WIDTH), F32)
    for c in range(LOADS):
        for load in loads[c]:
            load.wait()
        now = pl.ds(c * STEP, STEP)
        total = total + jnp.dot(maps[:, now], basis[now, :], preferred_element_type=F32)
    turned = total.T.reshape(NZ, RANK, ROWS)
    part_wide[...] = turned
    part[...] = turned.astype(BF16)
    for d in FAR:
        send_part(d).start()

    @pl.when(jnp.logical_not(owner))
    def _():
        send_part(0).start()

    whole = (ROWS, ROWS)
    eye = lax.broadcasted_iota(jnp.int32, whole, 0) == lax.broadcasted_iota(jnp.int32, whole, 1)
    spread = jnp.where(eye, jnp.broadcast_to(noise_ref[...], whole), 0.0)
    noise = jnp.sum(spread, axis=1, keepdims=True)

    @pl.loop(0, CELLS // PAIR)
    def _(c):
        now = pl.ds(pl.multiple_of(c * PAIR, PAIR), PAIR)
        base[:, now] = noise * maps[:, now].astype(F32)
        basis_t[:, now] = basis[now, :].T

    @pl.when(owner)
    def _():
        length = len_ref[pl.ds(z, 1), :]
        square = (DIN, DIN)
        eye = lax.broadcasted_iota(jnp.int32, square, 0) == lax.broadcasted_iota(jnp.int32, square, 1)
        column = jnp.sum(jnp.where(eye, jnp.broadcast_to(length, square), 0.0), axis=1, keepdims=True)
        inverse = 1.0 / column
        squared = inverse * inverse
        lanes = lax.broadcasted_iota(jnp.int32, (1, NZ), 1)
        amp = jnp.sum(jnp.where(lanes == z, amp_ref[...], 0.0), axis=1, keepdims=True)
        index = lax.broadcasted_iota(jnp.int32, (DIN, PAIR), 0)

        def halves(inputs):
            scaled = inputs * inverse
            return split3(0.5 * jnp.sum(scaled * scaled, axis=0, keepdims=True))

        def both(ref, slot):
            return jnp.concatenate([ref[slot, 0], ref[slot, 1]], 1)

        for d in range(NY):
            for to in range(NC):
                if d or not to:
                    got(ROW, d, to, rows_x.at[d, to])
        cols_x[0] = rows_x[0]
        for d in range(NY):
            inputs = both(rows_x, d)
            ha, hb, hc = halves(inputs)
            wa, wb, wc = split3(inputs * squared)
            tail = pick(index, -ha, -hb, -hc, -1.0, -1.0, -1.0)
            side[:, d * PAIR:(d + 1) * PAIR] = jnp.concatenate([wa, wb, wc, tail], 0).astype(BF16)
        for d in range(NX):
            if d:
                for to in range(NC):
                    got(COL, d, to, cols_x.at[d, to])
            inputs = both(cols_x, d)
            ha, hb, hc = halves(inputs)
            tail = pick(index, 1.0, 1.0, 1.0, ha, hb, hc)
            left[d] = jnp.concatenate([inputs, inputs, inputs, tail], 0).T.astype(BF16)

        own = [jnp.zeros((RANK, ROWS), F32), part_wide[z]]
        for d in (0, 1, 7, 2, 6, 3, 5, 4):
            for to in range(NC):
                if d or not to:
                    got(PART, d, to, part_in.at[d, to])
                    own[to] = own[to] + part_in[d, to].astype(F32)
        for to in range(NC):
            proj[0, to] = own[to].astype(BF16)
        for d in (2, 1, 3):
            send_proj(d).start()

        @pl.loop(0, NX * NC)
        def _(step):
            d, half = step // NC, step % NC
            now = pl.ds(pl.multiple_of(half * (NY * ROWS), NY * ROWS), NY * ROWS)
            logit = jnp.dot(left[d], side[:, now], preferred_element_type=F32)
            tile[d, :, now] = (amp * jnp.exp(jnp.minimum(logit, 0.0))).astype(BF16)

        for d in (1, 3, 2):
            got(PROJ, d, 0, proj.at[d])
        blocks = [both(proj, d) for d in range(NX)]
        for d in (*FAR, 0):
            now = pl.ds(d * PAIR, PAIR)
            values = jnp.zeros((RANK, PAIR), F32)
            for e in range(NX):
                values = values + jnp.dot(blocks[e], tile[e, :, now], preferred_element_type=F32)
            if d:
                sums[d, 0] = values[:, :ROWS].astype(BF16)
                sums[d, 1] = values[:, ROWS:].astype(BF16)
                send_sum(d).start()
        final = [values[:, :ROWS], values[:, ROWS:]]
        for d in (1, 7, 2, 6, 3, 5, 4):
            got(SUM, d, 0, sums_in.at[d])
            for to in range(NC):
                final[to] = final[to] + sums_in[d, to].astype(F32)
        for to in range(NC):
            lat_src[to] = final[to].astype(BF16)
        latent[z] = final[1].astype(BF16)
        for d in FAR:
            send_latent(d, 0).start()
            send_latent(d, 1).start()
        send_latent(0, 0).start()

        for d in (1, 7, 2, 6, 3, 5, 4):
            got(LAT1, d, 0, latent.at[(z + NZ - d) % NZ])

    @pl.when(jnp.logical_not(owner))
    def _():
        for d in (0, 1, 7, 2, 6, 3, 5, 4):
            got(LAT0, d, 0, latent.at[(z + NZ - d) % NZ])

    mixed = latent[...].reshape(WIDTH, ROWS).astype(F32).T.astype(BF16)
    for c in range(LOADS):
        now = pl.ds(c * STEP, STEP)
        expand = jnp.dot(mixed, basis_t[:, now], preferred_element_type=F32)
        out_ref[:, now] = (expand + base[:, now]).astype(BF16)

    for d in FAR:
        send_row(d).wait_send()
        send_part(d).wait_send()
    for d in (1, 2, 3):
        send_col(d).wait_send()

    @pl.when(owner)
    def _():
        for d in (1, 2, 3):
            send_proj(d).wait_send()
        for d in FAR:
            send_sum(d).wait_send()
            send_latent(d, 1).wait_send()
            send_latent(d, 0).wait_send()
        send_latent(0, 0).wait_send()

    @pl.when(jnp.logical_not(owner))
    def _():
        send_row(0).wait_send()
        send_part(0).wait_send()


def shards(maps, run_inputs, basis, amplitude, length, noise):
    operands = (run_inputs, amplitude.reshape(1, NZ), length, noise.reshape(1, ROWS), maps, basis)
    operands = [pltpu.with_memory_space_constraint(a, pltpu.HBM) for a in operands]
    hbm = pl.BlockSpec(memory_space=pltpu.HBM)
    return pl.pallas_call(
        kernel,
        out_shape=pltpu.VMEM((ROWS, CELLS), BF16),
        in_specs=[hbm] * 6,
        out_specs=pl.BlockSpec(memory_space=pltpu.VMEM),
        scratch_shapes=[
            pltpu.VMEM((DIN, ROWS), BF16),
            pltpu.VMEM((1, NZ), F32),
            pltpu.VMEM((NZ, DIN), F32),
            pltpu.VMEM((1, ROWS), F32),
            pltpu.VMEM((ROWS, CELLS), BF16),
            pltpu.VMEM((CELLS, WIDTH), BF16),
            pltpu.VMEM((WIDTH, CELLS), BF16),
            pltpu.VMEM((ROWS, CELLS), F32),
            pltpu.VMEM((DIN, ROWS), F32),
            pltpu.VMEM((NY, NC, DIN, ROWS), F32),
            pltpu.VMEM((NX, NC, DIN, ROWS), F32),
            pltpu.VMEM((NZ, RANK, ROWS), F32),
            pltpu.VMEM((NZ, RANK, ROWS), BF16),
            pltpu.VMEM((NZ, NC, RANK, ROWS), BF16),
            pltpu.VMEM((NX, NC, RANK, ROWS), BF16),
            pltpu.VMEM((NX, PAIR, RANK), BF16),
            pltpu.VMEM((RANK, NY * PAIR), BF16),
            pltpu.VMEM((NX, PAIR, NY * PAIR), BF16),
            pltpu.VMEM((NY, NC, RANK, ROWS), BF16),
            pltpu.VMEM((NY, NC, RANK, ROWS), BF16),
            pltpu.VMEM((NC, RANK, ROWS), BF16),
            pltpu.VMEM((NZ, RANK, ROWS), BF16),
            pltpu.SemaphoreType.DMA((3, LOADS)),
            pltpu.SemaphoreType.DMA((7, 8)),
            pltpu.SemaphoreType.DMA((7, 8, NC)),
        ],
        compiler_params=pltpu.CompilerParams(
            collective_id=0, has_side_effects=True, vmem_limit_bytes=32 * 1024 * 1024
        ),
    )(*operands)


def solution(mesh):
    in_specs = (P("runs", "cells"), P(None, "runs"), P("cells", None), P(), P(), P("runs"))
    out_specs = P("runs", "cells")
    return jax.shard_map(shards, mesh=mesh, in_specs=in_specs, out_specs=out_specs, check_vma=False)
```

time: 231 us -> 34.8 us (0.15)
  blocking collectives: 89.7 us -> 0 us
  matrix products: 86 us -> 0 us
  Pallas kernels: 0 us -> 33.9 us
  waiting for transfers between devices: 24.3 us -> 0 us
  between operations: 13.5 us -> 0.01 us
  local copies, waits for them, and re-layouts: 12.1 us -> 0.8 us
  other arithmetic: 4.09 us -> 0 us
    dot_general x18 -> x0, matrix products: 86 us -> none  [the longest x8 71.3 us: step(): jnp.einsum('qdr,qdc->qrc', rows_scaled, scaled_now, precision=lax.Precisi...]
    all_gather x1 -> x0, blocking collectives: 58.4 us -> none  [shards(): lax.all_gather(run_inputs, 'runs', axis=1, tiled=True)]
    pallas_call x0 -> x1, Pallas kernels: none -> 33.9 us  [shards(): pl.pallas_call(kernel, out_shape=pltpu.VMEM((ROWS, CELLS), BF16), in_spec...]
    psum x1 -> x0, blocking collectives: 31.3 us -> none  [shards(): summed = lax.psum(partial_proj, 'cells')]
    all_gather x1 -> x0, waiting for transfers between devices: 24.3 us -> none  [shards(): lax.all_gather(projected, 'runs', axis=1, tiled=True)]
    unnamed x9 -> x1, local copies, waits for them, and re-layouts: 7.75 us -> 0.8 us
    reshape x1 -> x0, local copies, waits for them, and re-layouts: 4.25 us -> none  [fold(): proj_piece.reshape(owned, rank, count, block).transpose(2, 0, 1, 3)]
  transfers between devices with their start and end apart: 1 -> 0, of which waited for: 1 -> 0; matrix products, arithmetic and copies ran while one was open for 2% -> 0% of each run, Pallas kernels for 0% -> 0%
where the time goes in v2:
time: 34.8 us; the launch traced here: 34.7 us
  Pallas kernels  33.9 us (97%)
  local copies, waits for them, and re-layouts  0.8 us (2%)
    pallas_call x1, Pallas kernels, shards(): pl.pallas_call(kernel, out_shape=pltpu.VMEM((ROWS, CELLS), BF16), in_spec...  33.9 us
    unnamed x1, local copies, waits for them, and re-layouts  0.8 us

profile of v2, /device:TPU:1, one launch (start us, length us, event | category | flops | bytes accessed | tf_op | source)
XLA Modules:
  0.0 34.7 jit_solution(3876668784733038577)
XLA Ops:
  0.0 33.9 %shard_map.64 = bf16[128,2048]{1,0:T(8,128)(2,1)S(1)} custom-call(bf16[8,128]{1,0:T(8,128)(2,1)} %x_hbm.1, f32[1,8]{1,0:T(1,128)} %bitcast.2, f32[8,8]{1,0:T(8,128)} %len_hbm.1, f32[1,128]{1,0:T(1,128)} %bitcast.3, bf16[128,2048]{1,0:T(8,128)(2,1)} %maps_hbm.1, bf16[2048,256]{1,0:T(8,128)(2,1)} %basis_hbm.1), custom_call_target="tpu_custom_call" | custom-call | tf_op jit(solution)/shard_map/pallas_call | solution.py:288
  33.9 0.8 %copy.8 = bf16[128,2048]{1,0:T(8,128)(2,1)} copy(bf16[128,2048]{1,0:T(8,128)(2,1)S(1)} %shard_map.64) | data formatting | bytes 1048576

commit v3 on v2

v3 whole, which is shorter than its diff:
```python
import jax
import jax.numpy as jnp
from jax import lax
from jax.experimental import pallas as pl
from jax.experimental.pallas import tpu as pltpu
from jax.sharding import PartitionSpec as P

MESH = pl.DeviceIdType.MESH
F32 = jnp.float32
BF16 = jnp.bfloat16
NY, NX, NC, NZ = 8, 4, 2, 8
ROWS = 128
PAIR = NC * ROWS
RANK = 32
DIN = 8
CELLS = 2048
WIDTH = NZ * RANK
LOADS = 4
STEP = CELLS // LOADS
FAR = (4, 3, 5, 2, 6, 1, 7)
ROW, COL, PART, PROJ, SUM, LAT0, LAT1 = range(7)


def split3(value):
    high = value.astype(BF16).astype(F32)
    rest = value - high
    mid = rest.astype(BF16).astype(F32)
    return high, mid, rest - mid


def pick(index, *values):
    out = jnp.zeros(index.shape, F32)
    for place, value in enumerate(values):
        out = jnp.where(index == place, value, out)
    return out


def kernel(
    x_hbm, amp_hbm, len_hbm, noise_hbm, maps_hbm, basis_hbm, out_ref,
    x_ref, amp_ref, len_ref, noise_ref, maps, basis, basis_t, base, mine, rows_x, cols_x,
    part_wide, part, part_in, proj, left, side, tile, sums, sums_in, lat_src, latent,
    load_sem, send_sem, recv_sem,
):
    run = lax.axis_index("runs")
    z = lax.axis_index("cells")
    y, x, core = run // (NX * NC), (run // NC) % NX, run % NC
    owner = core == 1

    def at(dy, dx, to, dz):
        place = ((y + dy + NY) % NY) * (NX * NC) + ((x + dx + NX) % NX) * NC + to
        return (place, (z + dz + NZ) % NZ)

    barrier = pltpu.get_barrier_semaphore()

    def greet(device):
        pl.semaphore_signal(barrier, inc=1, device_id=device, device_id_type=MESH)

    @pl.when(owner)
    def _():
        for d in FAR:
            for to in range(NC):
                greet(at(0, 0, to, d))

    @pl.when(jnp.logical_not(owner))
    def _():
        for d in (*FAR, 0):
            greet(at(0, 0, 1, d))

    loads = []
    for c in range(LOADS):
        now = pl.ds(c * STEP, STEP)
        loads.append((
            pltpu.make_async_copy(maps_hbm.at[:, now], maps.at[:, now], load_sem.at[0, c]),
            pltpu.make_async_copy(basis_hbm.at[now], basis.at[now], load_sem.at[1, c]),
        ))
    small = [
        pltpu.make_async_copy(source, target, load_sem.at[2, place])
        for place, (source, target) in enumerate(
            ((x_hbm, x_ref), (len_hbm, len_ref), (amp_hbm, amp_ref), (noise_hbm, noise_ref))
        )
    ]
    for load in (*loads[0], *loads[1], *loads[2], *loads[3], *small):
        load.start()

    @pl.when(owner)
    def _():
        for d in FAR:
            for to in range(NC):
                greet(at(d, 0, to, 0))
        for d in (2, 1, 3):
            for to in range(NC):
                greet(at(0, d, to, 0))
        greet(at(0, 0, 0, 0))

    def remote(phase, source, target, device):
        return pltpu.make_async_remote_copy(
            src_ref=source, dst_ref=target, send_sem=send_sem.at[phase],
            recv_sem=recv_sem.at[phase], device_id=device, device_id_type=MESH,
        )

    def received(phase, target):
        remote(phase, target, target, at(0, 0, 1, 1)).wait_recv()

    def left_here(phase, source):
        remote(phase, source, source, at(0, 0, 1, 1)).wait_send()

    def send_row(d):
        remote(ROW, mine, rows_x.at[d * NC + core], at(d, 0, 1, 0)).start()

    def send_part(d):
        remote(PART, part.at[(z + d) % NZ], part_in.at[d * NC + core], at(0, 0, 1, d)).start()

    total = jnp.zeros((ROWS, WIDTH), F32)
    for c in range(LOADS):
        for load in loads[c]:
            load.wait()
        now = pl.ds(c * STEP, STEP)
        total = total + jnp.dot(maps[:, now], basis[now, :], preferred_element_type=F32)
    turned = total.T.reshape(NZ, RANK, ROWS)
    part_wide[...] = turned
    part[...] = turned.astype(BF16)
    for load in small:
        load.wait()
    mine[...] = x_ref[...].astype(F32)

    @pl.when(owner)
    def _():
        pl.semaphore_wait(barrier, 25)

    @pl.when(jnp.logical_not(owner))
    def _():
        pl.semaphore_wait(barrier, 18)

    for d in FAR:
        send_part(d)
    for d in FAR:
        send_row(d)
    for d in (2, 1, 3):
        remote(COL, mine, cols_x.at[d * NC + core], at(0, d, 1, 0)).start()

    @pl.when(jnp.logical_not(owner))
    def _():
        send_part(0)
        send_row(0)

    whole = (ROWS, ROWS)
    eye = lax.broadcasted_iota(jnp.int32, whole, 0) == lax.broadcasted_iota(jnp.int32, whole, 1)
    spread = jnp.where(eye, jnp.broadcast_to(noise_ref[...], whole), 0.0)
    noise = jnp.sum(spread, axis=1, keepdims=True)

    @pl.loop(0, CELLS // PAIR)
    def _(c):
        now = pl.ds(pl.multiple_of(c * PAIR, PAIR), PAIR)
        base[:, now] = noise * maps[:, now].astype(F32)
        basis_t[:, now] = basis[now, :].T

    @pl.when(owner)
    def _():
        length = len_ref[pl.ds(z, 1), :]
        square = (DIN, DIN)
        eye = lax.broadcasted_iota(jnp.int32, square, 0) == lax.broadcasted_iota(jnp.int32, square, 1)
        column = jnp.sum(jnp.where(eye, jnp.broadcast_to(length, square), 0.0), axis=1, keepdims=True)
        inverse = 1.0 / column
        squared = inverse * inverse
        lanes = lax.broadcasted_iota(jnp.int32, (1, NZ), 1)
        amp = jnp.sum(jnp.where(lanes == z, amp_ref[...], 0.0), axis=1, keepdims=True)

        def halves(inputs):
            scaled = inputs * inverse
            return split3(0.5 * jnp.sum(scaled * scaled, axis=0, keepdims=True))

        def side_by_side(ref, count):
            return jnp.concatenate([ref[k] for k in range(count)], 1)

        def place(count):
            return lax.broadcasted_iota(jnp.int32, (DIN, count), 0)

        received(PART, part_in.at[pl.ds(0, NZ * NC - 1)])
        own = [part_in[0].astype(F32), part_wide[z]]
        for d in range(1, NZ):
            for to in range(NC):
                own[to] = own[to] + part_in[d * NC + to].astype(F32)
        for to in range(NC):
            proj[0, to] = own[to].astype(BF16)
        for d in (2, 1, 3):
            remote(PROJ, proj.at[0], proj.at[d], at(0, d, 1, 0)).start()

        received(ROW, rows_x.at[pl.ds(0, NY * NC - 1)])
        rows_x[1] = mine[...]
        inputs = side_by_side(rows_x, NY * NC)
        ha, hb, hc = halves(inputs)
        wa, wb, wc = split3(inputs * squared)
        tail = pick(place(NY * PAIR), -ha, -hb, -hc, -1.0, -1.0, -1.0)
        side[...] = jnp.concatenate([wa, wb, wc, tail], 0).astype(BF16)
        received(COL, cols_x.at[pl.ds(0, (NX - 1) * NC)])
        for to in range(NC):
            cols_x[to] = rows_x[to]
        inputs = side_by_side(cols_x, NX * NC)
        ha, hb, hc = halves(inputs)
        tail = pick(place(NX * PAIR), 1.0, 1.0, 1.0, ha, hb, hc)
        left[...] = jnp.concatenate([inputs, inputs, inputs, tail], 0).T.astype(BF16)

        @pl.loop(0, NX)
        def _(d):
            now = pl.ds(pl.multiple_of(d * PAIR, PAIR), PAIR)
            logit = jnp.dot(left[now, :], side[...], preferred_element_type=F32)
            tile[d] = (amp * jnp.exp(jnp.minimum(logit, 0.0))).astype(BF16)

        received(PROJ, proj.at[pl.ds(1, NX - 1)])
        blocks = [jnp.concatenate([proj[d, 0], proj[d, 1]], 1) for d in range(NX)]
        for d in (*FAR, 0):
            now = pl.ds(d * PAIR, PAIR)
            values = jnp.zeros((RANK, PAIR), F32)
            for e in range(NX):
                values = values + jnp.dot(blocks[e], tile[e, :, now], preferred_element_type=F32)
            if d:
                sums[d, 0] = values[:, :ROWS].astype(BF16)
                sums[d, 1] = values[:, ROWS:].astype(BF16)
                remote(SUM, sums.at[d], sums_in.at[d], at(-d, 0, 1, 0)).start()
        received(SUM, sums_in.at[pl.ds(1, NY - 1)])
        final = [values[:, :ROWS], values[:, ROWS:]]
        for d in range(1, NY):
            for to in range(NC):
                final[to] = final[to] + sums_in[d, to].astype(F32)
        for to in range(NC):
            lat_src[to] = final[to].astype(BF16)
        for d in FAR:
            remote(LAT1, lat_src.at[1], latent.at[z], at(0, 0, 1, d)).start()
            remote(LAT0, lat_src.at[0], latent.at[z], at(0, 0, 0, d)).start()
        remote(LAT0, lat_src.at[0], latent.at[z], at(0, 0, 0, 0)).start()
        latent[z] = lat_src[1]

        left_here(ROW, rows_x.at[pl.ds(0, NY - 1)])
        left_here(COL, cols_x.at[pl.ds(0, NX - 1)])
        left_here(PART, part.at[pl.ds(0, NZ - 1)])
        left_here(PROJ, proj.at[pl.ds(0, NX - 1)])
        left_here(SUM, sums.at[pl.ds(0, NY - 1)])
        left_here(LAT0, part)
        left_here(LAT1, part.at[pl.ds(0, NZ - 1)])
        received(LAT1, latent.at[pl.ds(0, NZ - 1)])

    @pl.when(jnp.logical_not(owner))
    def _():
        left_here(ROW, rows_x.at[pl.ds(0, NY)])
        left_here(COL, cols_x.at[pl.ds(0, NX - 1)])
        left_here(PART, part)
        received(LAT0, latent)

    mixed = latent[...].reshape(WIDTH, ROWS).astype(F32).T.astype(BF16)
    for c in range(LOADS):
        now = pl.ds(c * STEP, STEP)
        expand = jnp.dot(mixed, basis_t[:, now], preferred_element_type=F32)
        out_ref[:, now] = (expand + base[:, now]).astype(BF16)


def shards(maps, run_inputs, basis, amplitude, length, noise):
    operands = (run_inputs, amplitude.reshape(1, NZ), length, noise.reshape(1, ROWS), maps, basis)
    operands = [pltpu.with_memory_space_constraint(a, pltpu.HBM) for a in operands]
    hbm = pl.BlockSpec(memory_space=pltpu.HBM)
    return pl.pallas_call(
        kernel,
        out_shape=pltpu.VMEM((ROWS, CELLS), BF16),
        in_specs=[hbm] * 6,
        out_specs=pl.BlockSpec(memory_space=pltpu.VMEM),
        scratch_shapes=[
            pltpu.VMEM((DIN, ROWS), BF16),
            pltpu.VMEM((1, NZ), F32),
            pltpu.VMEM((NZ, DIN), F32),
            pltpu.VMEM((1, ROWS), F32),
            pltpu.VMEM((ROWS, CELLS), BF16),
            pltpu.VMEM((CELLS, WIDTH), BF16),
            pltpu.VMEM((WIDTH, CELLS), BF16),
            pltpu.VMEM((ROWS, CELLS), F32),
            pltpu.VMEM((DIN, ROWS), F32),
            pltpu.VMEM((NY * NC, DIN, ROWS), F32),
            pltpu.VMEM((NX * NC, DIN, ROWS), F32),
            pltpu.VMEM((NZ, RANK, ROWS), F32),
            pltpu.VMEM((NZ, RANK, ROWS), BF16),
            pltpu.VMEM((NZ * NC, RANK, ROWS), BF16),
            pltpu.VMEM((NX, NC, RANK, ROWS), BF16),
            pltpu.VMEM((NX * PAIR, RANK), BF16),
            pltpu.VMEM((RANK, NY * PAIR), BF16),
            pltpu.VMEM((NX, PAIR, NY * PAIR), BF16),
            pltpu.VMEM((NY, NC, RANK, ROWS), BF16),
            pltpu.VMEM((NY, NC, RANK, ROWS), BF16),
            pltpu.VMEM((NC, RANK, ROWS), BF16),
            pltpu.VMEM((NZ, RANK, ROWS), BF16),
            pltpu.SemaphoreType.DMA((3, LOADS)),
            pltpu.SemaphoreType.DMA((7,)),
            pltpu.SemaphoreType.DMA((7,)),
        ],
        compiler_params=pltpu.CompilerParams(
            collective_id=0, has_side_effects=True, vmem_limit_bytes=32 * 1024 * 1024
        ),
    )(*operands)


def solution(mesh):
    in_specs = (P("runs", "cells"), P(None, "runs"), P("cells", None), P(), P(), P("runs"))
    out_specs = P("runs", "cells")
    return jax.shard_map(shards, mesh=mesh, in_specs=in_specs, out_specs=out_specs, check_vma=False)
```

time: 34.8 us -> 32.6 us (0.937)
  Pallas kernels: 33.9 us -> 31.6 us
    pallas_call x1, Pallas kernels: 33.9 us -> 31.6 us  [shards(): pl.pallas_call(kernel, out_shape=pltpu.VMEM((ROWS, CELLS), BF16), in_spec...]
where the time goes in v3:
time: 32.6 us; the launch traced here: 32.4 us
  Pallas kernels  31.6 us (97%)
  local copies, waits for them, and re-layouts  0.8 us (2%)
    pallas_call x1, Pallas kernels, shards(): pl.pallas_call(kernel, out_shape=pltpu.VMEM((ROWS, CELLS), BF16), in_spec...  31.6 us
    unnamed x1, local copies, waits for them, and re-layouts  0.8 us

profile of v3, /device:TPU:1, one launch (start us, length us, event | category | flops | bytes accessed | tf_op | source)
XLA Modules:
  0.0 32.4 jit_solution(11011168187357928841)
XLA Ops:
  0.0 31.6 %shard_map.64 = bf16[128,2048]{1,0:T(8,128)(2,1)S(1)} custom-call(bf16[8,128]{1,0:T(8,128)(2,1)} %x_hbm.1, f32[1,8]{1,0:T(1,128)} %bitcast.2, f32[8,8]{1,0:T(8,128)} %len_hbm.1, f32[1,128]{1,0:T(1,128)} %bitcast.3, bf16[128,2048]{1,0:T(8,128)(2,1)} %maps_hbm.1, bf16[2048,256]{1,0:T(8,128)(2,1)} %basis_hbm.1), custom_call_target="tpu_custom_call" | custom-call | tf_op jit(solution)/shard_map/pallas_call | solution.py:260
  31.7 0.8 %copy.8 = bf16[128,2048]{1,0:T(8,128)(2,1)} copy(bf16[128,2048]{1,0:T(8,128)(2,1)S(1)} %shard_map.64) | data formatting | bytes 1048576

commit v4 on v3

--- a/solution.py
+++ b/solution.py
@@ -10,6 +10,7 @@
 BF16 = jnp.bfloat16
 NY, NX, NC, NZ = 8, 4, 2, 8
 ROWS = 128
+HALF = NZ // 2
 PAIR = NC * ROWS
 RANK = 32
 DIN = 8
@@ -18,7 +19,7 @@
 LOADS = 4
 STEP = CELLS // LOADS
 FAR = (4, 3, 5, 2, 6, 1, 7)
-ROW, COL, PART, PROJ, SUM, LAT0, LAT1 = range(7)
+ROW, COL, PART, PROJ, SUM, LAT0, LAT1, RELAY = range(8)
 
 
 def split3(value):
@@ -38,13 +39,15 @@
 def kernel(
     x_hbm, amp_hbm, len_hbm, noise_hbm, maps_hbm, basis_hbm, out_ref,
     x_ref, amp_ref, len_ref, noise_ref, maps, basis, basis_t, base, mine, rows_x, cols_x,
-    part_wide, part, part_in, proj, left, side, tile, sums, sums_in, lat_src, latent,
+    part_wide, part, relay, part_in, proj, left, side, tile, sums, sums_in, lat_src, latent,
     load_sem, send_sem, recv_sem,
 ):
     run = lax.axis_index("runs")
     z = lax.axis_index("cells")
     y, x, core = run // (NX * NC), (run // NC) % NX, run % NC
     owner = core == 1
+    early = z < HALF
+    late = jnp.logical_not(early)
 
     def at(dy, dx, to, dz):
         place = ((y + dy + NY) % NY) * (NX * NC) + ((x + dx + NX) % NX) * NC + to
@@ -58,13 +61,11 @@
     @pl.when(owner)
     def _():
         for d in FAR:
-            for to in range(NC):
-                greet(at(0, 0, to, d))
-
-    @pl.when(jnp.logical_not(owner))
-    def _():
-        for d in (*FAR, 0):
             greet(at(0, 0, 1, d))
+
+            @pl.when(jnp.logical_or(early, (z + d) % NZ >= HALF))
+            def _():
+                greet(at(0, 0, 0, d))
 
     loads = []
     for c in range(LOADS):
@@ -92,9 +93,9 @@
                 greet(at(0, d, to, 0))
         greet(at(0, 0, 0, 0))
 
-    def remote(phase, source, target, device):
+    def remote(phase, source, target, device, away=None):
         return pltpu.make_async_remote_copy(
-            src_ref=source, dst_ref=target, send_sem=send_sem.at[phase],
+            src_ref=source, dst_ref=target, send_sem=send_sem.at[phase if away is None else away],
             recv_sem=recv_sem.at[phase], device_id=device, device_id_type=MESH,
         )
 
@@ -107,8 +108,15 @@
     def send_row(d):
         remote(ROW, mine, rows_x.at[d * NC + core], at(d, 0, 1, 0)).start()
 
-    def send_part(d):
-        remote(PART, part.at[(z + d) % NZ], part_in.at[d * NC + core], at(0, 0, 1, d)).start()
+    def send_part(q):
+        slot = (q - z + NZ) % NZ
+        remote(PART, part.at[q], part_in.at[slot * NC + core], at(0, 0, 1, q - z)).start()
+
+    def send_parts(first, last):
+        for q in range(first, last):
+            @pl.when(jnp.logical_or(core == 0, z != q))
+            def _():
+                send_part(q)
 
     total = jnp.zeros((ROWS, WIDTH), F32)
     for c in range(LOADS):
@@ -123,25 +131,44 @@
         load.wait()
     mine[...] = x_ref[...].astype(F32)
 
+    @pl.when(jnp.logical_not(owner))
+    def _():
+        @pl.when(early)
+        def _():
+            pl.semaphore_wait(barrier, 14)
+            remote(RELAY, part.at[pl.ds(HALF, HALF)], relay.at[:, 0], at(0, 0, 1, 0)).start()
+
+        @pl.when(late)
+        def _():
+            pl.semaphore_wait(barrier, 18)
+
+        send_row(0)
+
     @pl.when(owner)
     def _():
-        pl.semaphore_wait(barrier, 25)
-
-    @pl.when(jnp.logical_not(owner))
-    def _():
-        pl.semaphore_wait(barrier, 18)
-
-    for d in FAR:
-        send_part(d)
+        @pl.when(early)
+        def _():
+            relay[:, 1] = part[HALF:]
+            received(RELAY, part.at[pl.ds(0, HALF)])
+
+        pl.semaphore_wait(barrier, 17)
+
+        @pl.when(early)
+        def _():
+            for q in range(HALF, NZ):
+                slot = (q - z + NZ) % NZ
+                place = part_in.at[pl.ds(slot * NC, NC)]
+                remote(PART, relay.at[q - HALF], place, at(0, 0, 1, q - z), RELAY).start()
+
+    @pl.when(late)
+    def _():
+        send_parts(HALF, NZ)
+
+    send_parts(0, HALF)
     for d in FAR:
         send_row(d)
     for d in (2, 1, 3):
         remote(COL, mine, cols_x.at[d * NC + core], at(0, d, 1, 0)).start()
-
-    @pl.when(jnp.logical_not(owner))
-    def _():
-        send_part(0)
-        send_row(0)
 
     whole = (ROWS, ROWS)
     eye = lax.broadcasted_iota(jnp.int32, whole, 0) == lax.broadcasted_iota(jnp.int32, whole, 1)
@@ -208,15 +235,21 @@
 
         received(PROJ, proj.at[pl.ds(1, NX - 1)])
         blocks = [jnp.concatenate([proj[d, 0], proj[d, 1]], 1) for d in range(NX)]
-        for d in (*FAR, 0):
-            now = pl.ds(d * PAIR, PAIR)
+        def product(slot):
+            now = pl.ds(pl.multiple_of(slot * PAIR, PAIR), PAIR)
             values = jnp.zeros((RANK, PAIR), F32)
             for e in range(NX):
                 values = values + jnp.dot(blocks[e], tile[e, :, now], preferred_element_type=F32)
-            if d:
-                sums[d, 0] = values[:, :ROWS].astype(BF16)
-                sums[d, 1] = values[:, ROWS:].astype(BF16)
-                remote(SUM, sums.at[d], sums_in.at[d], at(-d, 0, 1, 0)).start()
+            return values
+
+        for step in range(NY - 1):
+            to_y = step + (step >= y).astype(jnp.int32)
+            slot = (y - to_y + NY) % NY
+            values = product(slot)
+            sums[slot, 0] = values[:, :ROWS].astype(BF16)
+            sums[slot, 1] = values[:, ROWS:].astype(BF16)
+            remote(SUM, sums.at[slot], sums_in.at[slot], at(to_y - y, 0, 1, 0)).start()
+        values = product(0)
         received(SUM, sums_in.at[pl.ds(1, NY - 1)])
         final = [values[:, :ROWS], values[:, ROWS:]]
         for d in range(1, NY):
@@ -224,15 +257,24 @@
                 final[to] = final[to] + sums_in[d, to].astype(F32)
         for to in range(NC):
             lat_src[to] = final[to].astype(BF16)
-        for d in FAR:
-            remote(LAT1, lat_src.at[1], latent.at[z], at(0, 0, 1, d)).start()
-            remote(LAT0, lat_src.at[0], latent.at[z], at(0, 0, 0, d)).start()
         remote(LAT0, lat_src.at[0], latent.at[z], at(0, 0, 0, 0)).start()
+        for step in range(NZ - 1):
+            away = step + (step >= z).astype(jnp.int32) - z
+            remote(LAT1, lat_src.at[1], latent.at[z], at(0, 0, 1, away)).start()
+            remote(LAT0, lat_src.at[0], latent.at[z], at(0, 0, 0, away)).start()
         latent[z] = lat_src[1]
 
         left_here(ROW, rows_x.at[pl.ds(0, NY - 1)])
         left_here(COL, cols_x.at[pl.ds(0, NX - 1)])
-        left_here(PART, part.at[pl.ds(0, NZ - 1)])
+        @pl.when(early)
+        def _():
+            left_here(PART, part.at[pl.ds(0, HALF - 1)])
+            left_here(RELAY, part)
+
+        @pl.when(late)
+        def _():
+            left_here(PART, part.at[pl.ds(0, NZ - 1)])
+
         left_here(PROJ, proj.at[pl.ds(0, NX - 1)])
         left_here(SUM, sums.at[pl.ds(0, NY - 1)])
         left_here(LAT0, part)
@@ -243,7 +285,15 @@
     def _():
         left_here(ROW, rows_x.at[pl.ds(0, NY)])
         left_here(COL, cols_x.at[pl.ds(0, NX - 1)])
-        left_here(PART, part)
+        @pl.when(early)
+        def _():
+            left_here(PART, part.at[pl.ds(0, HALF)])
+            left_here(RELAY, part.at[pl.ds(0, HALF)])
+
+        @pl.when(late)
+        def _():
+            left_here(PART, part)
+
         received(LAT0, latent)
 
     mixed = latent[...].reshape(WIDTH, ROWS).astype(F32).T.astype(BF16)
@@ -276,6 +326,7 @@
             pltpu.VMEM((NX * NC, DIN, ROWS), F32),
             pltpu.VMEM((NZ, RANK, ROWS), F32),
             pltpu.VMEM((NZ, RANK, ROWS), BF16),
+            pltpu.VMEM((HALF, NC, RANK, ROWS), BF16),
             pltpu.VMEM((NZ * NC, RANK, ROWS), BF16),
             pltpu.VMEM((NX, NC, RANK, ROWS), BF16),
             pltpu.VMEM((NX * PAIR, RANK), BF16),
@@ -286,8 +337,8 @@
             pltpu.VMEM((NC, RANK, ROWS), BF16),
             pltpu.VMEM((NZ, RANK, ROWS), BF16),
             pltpu.SemaphoreType.DMA((3, LOADS)),
-            pltpu.SemaphoreType.DMA((7,)),
-            pltpu.SemaphoreType.DMA((7,)),
+            pltpu.SemaphoreType.DMA((8,)),
+            pltpu.SemaphoreType.DMA((8,)),
         ],
         compiler_params=pltpu.CompilerParams(
             collective_id=0, has_side_effects=True, vmem_limit_bytes=32 * 1024 * 1024

time: 32.6 us -> 32 us (0.982)
  Pallas kernels: 31.6 us -> 31.1 us
    pallas_call x1, Pallas kernels: 31.6 us -> 31.1 us  [shards(): pl.pallas_call(kernel, out_shape=pltpu.VMEM((ROWS, CELLS), BF16), in_spec...]
where the time goes in v4:
time: 32 us; the launch traced here: 31.9 us
  Pallas kernels  31.1 us (97%)
  local copies, waits for them, and re-layouts  0.8 us (2%)
    pallas_call x1, Pallas kernels, shards(): pl.pallas_call(kernel, out_shape=pltpu.VMEM((ROWS, CELLS), BF16), in_spec...  31.1 us
    unnamed x1, local copies, waits for them, and re-layouts  0.8 us

profile of v4, /device:TPU:1, one launch (start us, length us, event | category | flops | bytes accessed | tf_op | source)
XLA Modules:
  0.0 31.9 jit_solution(6976950538997961869)
XLA Ops:
  0.0 31.1 %shard_map.64 = bf16[128,2048]{1,0:T(8,128)(2,1)S(1)} custom-call(bf16[8,128]{1,0:T(8,128)(2,1)} %x_hbm.1, f32[1,8]{1,0:T(1,128)} %bitcast.2, f32[8,8]{1,0:T(8,128)} %len_hbm.1, f32[1,128]{1,0:T(1,128)} %bitcast.3, bf16[128,2048]{1,0:T(8,128)(2,1)} %maps_hbm.1, bf16[2048,256]{1,0:T(8,128)(2,1)} %basis_hbm.1), custom_call_target="tpu_custom_call" | custom-call | tf_op jit(solution)/shard_map/pallas_call | solution.py:310
  31.1 0.8 %copy.8 = bf16[128,2048]{1,0:T(8,128)(2,1)} copy(bf16[128,2048]{1,0:T(8,128)(2,1)S(1)} %shard_map.64) | data formatting | bytes 1048576

commit v5 on v3

v5 whole, which is shorter than its diff:
```python
import jax
import jax.numpy as jnp
from jax import lax
from jax.experimental import pallas as pl
from jax.experimental.pallas import tpu as pltpu
from jax.sharding import PartitionSpec as P

MESH = pl.DeviceIdType.MESH
F32 = jnp.float32
BF16 = jnp.bfloat16
NY, NX, NC, NZ = 8, 4, 2, 8
ROWS = 128
OWNERS = 4
EACH = NZ // OWNERS
PAIR = NC * ROWS
RANK = 32
DIN = 8
CELLS = 2048
WIDTH = NZ * RANK
LOADS = 2
STEP = CELLS // LOADS
FAR = (4, 3, 5, 2, 6, 1, 7)
ROW, COL, PART, PROJ, SUM, LAT0, LAT1 = range(7)


def split3(value):
    high = value.astype(BF16).astype(F32)
    rest = value - high
    mid = rest.astype(BF16).astype(F32)
    return high, mid, rest - mid


def pick(index, *values):
    out = jnp.zeros(index.shape, F32)
    for place, value in enumerate(values):
        out = jnp.where(index == place, value, out)
    return out


def kernel(
    x_hbm, amp_hbm, len_hbm, noise_hbm, maps_hbm, basis_hbm, out_ref,
    x_ref, amp_ref, len_ref, noise_ref, maps, basis, basis_t, base, mine, rows_x, cols_x,
    part_wide, part, part_in, proj, left, side, tile, sums, sums_in, lat_src, latent,
    load_sem, send_sem, recv_sem,
):
    run = lax.axis_index("runs")
    z = lax.axis_index("cells")
    y, x, core = run // (NX * NC), (run // NC) % NX, run % NC
    early = z < OWNERS
    late = jnp.logical_not(early)
    owner = jnp.logical_and(core == 1, early)

    first = z * EACH

    def at(dy, dx, to, dz):
        place = ((y + dy + NY) % NY) * (NX * NC) + ((x + dx + NX) % NX) * NC + to
        return (place, (z + dz + NZ) % NZ)

    barrier = pltpu.get_barrier_semaphore()

    def greet(device):
        pl.semaphore_signal(barrier, inc=1, device_id=device, device_id_type=MESH)

    loads = []
    for c in range(LOADS):
        now = pl.ds(c * STEP, STEP)
        loads.append((
            pltpu.make_async_copy(maps_hbm.at[:, now], maps.at[:, now], load_sem.at[0, c]),
            pltpu.make_async_copy(basis_hbm.at[now], basis.at[now], load_sem.at[1, c]),
        ))
    small = [
        pltpu.make_async_copy(source, target, load_sem.at[2, place])
        for place, (source, target) in enumerate(
            ((x_hbm, x_ref), (len_hbm, len_ref), (amp_hbm, amp_ref), (noise_hbm, noise_ref))
        )
    ]
    for load in (*loads[0], *loads[1], *small):
        load.start()

    @pl.when(owner)
    def _():
        for d in FAR:
            for to in range(NC):
                greet(at(d, 0, to, 0))
        for d in (2, 1, 3):
            for to in range(NC):
                greet(at(0, d, to, 0))
        greet(at(0, 0, 0, 0))
        for d in FAR:
            for to in range(NC):
                greet(at(0, 0, to, d))

    def remote(phase, source, target, device):
        return pltpu.make_async_remote_copy(
            src_ref=source, dst_ref=target, send_sem=send_sem.at[phase],
            recv_sem=recv_sem.at[phase], device_id=device, device_id_type=MESH,
        )

    def received(phase, target):
        remote(phase, target, target, at(0, 0, 1, 1)).wait_recv()

    def left_here(phase, source):
        remote(phase, source, source, at(0, 0, 1, 1)).wait_send()

    def send_row(d):
        remote(ROW, mine, rows_x.at[d * NC + core], at(d, 0, 1, 0)).start()

    total = jnp.zeros((ROWS, WIDTH), F32)
    for c in range(LOADS):
        for load in loads[c]:
            load.wait()
        now = pl.ds(c * STEP, STEP)
        total = total + jnp.dot(maps[:, now], basis[now, :], preferred_element_type=F32)
    turned = total.T.reshape(NZ, RANK, ROWS)
    part_wide[...] = turned
    part[...] = turned.astype(BF16)

    @pl.when(late)
    def _():
        pl.semaphore_wait(barrier, OWNERS)

    @pl.when(jnp.logical_and(early, core == 0))
    def _():
        pl.semaphore_wait(barrier, OWNERS + NY + NX - 2)

    @pl.when(owner)
    def _():
        pl.semaphore_wait(barrier, OWNERS + NY + NX - 3)

    for step in range(OWNERS):
        plane = 3 - step

        @pl.when(jnp.logical_or(core == 0, z != plane))
        def _():
            slot = ((plane - z + NZ) % NZ) * NC + core
            source = part.at[pl.ds(plane * EACH, EACH)]
            remote(PART, source, part_in.at[slot], at(0, 0, 1, plane - z)).start()

    for load in small:
        load.wait()

    @pl.when(early)
    def _():
        mine[...] = x_ref[...].astype(F32)
        for d in FAR:
            send_row(d)
        for d in (2, 1, 3):
            remote(COL, mine, cols_x.at[d * NC + core], at(0, d, 1, 0)).start()

        @pl.when(core == 0)
        def _():
            send_row(0)

    whole = (ROWS, ROWS)
    eye = lax.broadcasted_iota(jnp.int32, whole, 0) == lax.broadcasted_iota(jnp.int32, whole, 1)
    spread = jnp.where(eye, jnp.broadcast_to(noise_ref[...], whole), 0.0)
    noise = jnp.sum(spread, axis=1, keepdims=True)

    @pl.loop(0, CELLS // PAIR)
    def _(c):
        now = pl.ds(pl.multiple_of(c * PAIR, PAIR), PAIR)
        base[:, now] = noise * maps[:, now].astype(F32)
        basis_t[:, now] = basis[now, :].T

    def side_by_side(ref, count):
        return jnp.concatenate([ref[k] for k in range(count)], 1)

    def place(count):
        return lax.broadcasted_iota(jnp.int32, (DIN, count), 0)

    def make_tile(slot):
        q = first + slot
        length = len_ref[pl.ds(q, 1), :]
        square = (DIN, DIN)
        eye = lax.broadcasted_iota(jnp.int32, square, 0) == lax.broadcasted_iota(jnp.int32, square, 1)
        column = jnp.sum(jnp.where(eye, jnp.broadcast_to(length, square), 0.0), axis=1, keepdims=True)
        inverse = 1.0 / column
        squared = inverse * inverse
        lanes = lax.broadcasted_iota(jnp.int32, (1, NZ), 1)
        amp = jnp.sum(jnp.where(lanes == q, amp_ref[...], 0.0), axis=1, keepdims=True)

        def halves(inputs):
            scaled = inputs * inverse
            return split3(0.5 * jnp.sum(scaled * scaled, axis=0, keepdims=True))

        inputs = side_by_side(rows_x, NY * NC)
        ha, hb, hc = halves(inputs)
        wa, wb, wc = split3(inputs * squared)
        last = pick(place(NY * PAIR), -ha, -hb, -hc, -1.0, -1.0, -1.0)
        side[...] = jnp.concatenate([wa, wb, wc, last], 0).astype(BF16)
        inputs = side_by_side(cols_x, NX * NC)
        ha, hb, hc = halves(inputs)
        last = pick(place(NX * PAIR), 1.0, 1.0, 1.0, ha, hb, hc)
        left[...] = jnp.concatenate([inputs, inputs, inputs, last], 0).T.astype(BF16)

        @pl.loop(0, NX)
        def _(d):
            now = pl.ds(pl.multiple_of(d * PAIR, PAIR), PAIR)
            logit = jnp.dot(left[now, :], side[...], preferred_element_type=F32)
            tile[slot, d] = (amp * jnp.exp(jnp.minimum(logit, 0.0))).astype(BF16)

    @pl.when(owner)
    def _():
        received(ROW, rows_x.at[pl.ds(0, NY * NC - 1)])
        rows_x[1] = mine[...]
        received(COL, cols_x.at[pl.ds(0, (NX - 1) * NC)])
        for to in range(NC):
            cols_x[to] = rows_x[to]
        make_tile(0)

        received(PART, part_in.at[pl.ds(0, NZ * NC - 1)])
        for slot in range(EACH):
            own = [part_in[0, slot].astype(F32), part_wide[first + slot]]
            for d in range(1, NZ):
                for to in range(NC):
                    own[to] = own[to] + part_in[d * NC + to, slot].astype(F32)
            for to in range(NC):
                proj[0, slot, to] = own[to].astype(BF16)
        for d in (2, 1, 3):
            remote(PROJ, proj.at[0], proj.at[d], at(0, d, 1, 0)).start()
        for slot in range(1, EACH):
            make_tile(slot)

        def product(row, slot):
            now = pl.ds(pl.multiple_of(row * PAIR, PAIR), PAIR)
            values = jnp.zeros((RANK, PAIR), F32)
            for e in range(NX):
                block = jnp.concatenate([proj[e, slot, 0], proj[e, slot, 1]], 1)
                values = values + jnp.dot(block, tile[slot, e, :, now], preferred_element_type=F32)
            return values

        received(PROJ, proj.at[pl.ds(1, NX - 1)])

        for step in range(NY - 1):
            to_y = step + (step >= y).astype(jnp.int32)
            row = (y - to_y + NY) % NY
            for slot in range(EACH):
                values = product(row, slot)
                for to in range(NC):
                    sums[row, slot, to] = values[:, to * ROWS:(to + 1) * ROWS].astype(BF16)
            remote(SUM, sums.at[row], sums_in.at[row], at(to_y - y, 0, 1, 0)).start()
        own = [product(0, slot) for slot in range(EACH)]
        received(SUM, sums_in.at[pl.ds(1, NY - 1)])
        for slot in range(EACH):
            for to in range(NC):
                final = own[slot][:, to * ROWS:(to + 1) * ROWS]
                for d in range(1, NY):
                    final = final + sums_in[d, slot, to].astype(F32)
                lat_src[to, slot] = final.astype(BF16)
        spot = latent.at[pl.ds(first, EACH)]
        remote(LAT0, lat_src.at[0], spot, at(0, 0, 0, 0)).start()
        for step in range(NZ - 1):
            away = step + (step >= z).astype(jnp.int32) - z
            remote(LAT1, lat_src.at[1], spot, at(0, 0, 1, away)).start()
            remote(LAT0, lat_src.at[0], spot, at(0, 0, 0, away)).start()
        for slot in range(EACH):
            latent[first + slot] = lat_src[1, slot]

        left_here(ROW, rows_x.at[pl.ds(0, NY - 1)])
        left_here(COL, cols_x.at[pl.ds(0, NX - 1)])
        left_here(PART, part.at[pl.ds(0, NZ - EACH)])
        left_here(PROJ, proj.at[pl.ds(1, NX - 1)])
        left_here(SUM, sums.at[pl.ds(0, NY - 1)])
        left_here(LAT0, part_in.at[pl.ds(0, NZ)])
        left_here(LAT1, part_in.at[pl.ds(0, NZ - 1)])
        received(LAT1, latent.at[pl.ds(0, NZ - EACH)])

    @pl.when(jnp.logical_not(owner))
    def _():
        left_here(PART, part)

        @pl.when(early)
        def _():
            left_here(ROW, rows_x.at[pl.ds(0, NY)])
            left_here(COL, cols_x.at[pl.ds(0, NX - 1)])

        @pl.when(core == 0)
        def _():
            received(LAT0, latent)

        @pl.when(core == 1)
        def _():
            received(LAT1, latent)

    mixed = latent[...].reshape(WIDTH, ROWS).astype(F32).T.astype(BF16)
    for c in range(LOADS):
        now = pl.ds(c * STEP, STEP)
        expand = jnp.dot(mixed, basis_t[:, now], preferred_element_type=F32)
        out_ref[:, now] = (expand + base[:, now]).astype(BF16)


def shards(maps, run_inputs, basis, amplitude, length, noise):
    operands = (run_inputs, amplitude.reshape(1, NZ), length, noise.reshape(1, ROWS), maps, basis)
    operands = [pltpu.with_memory_space_constraint(a, pltpu.HBM) for a in operands]
    hbm = pl.BlockSpec(memory_space=pltpu.HBM)
    return pl.pallas_call(
        kernel,
        out_shape=pltpu.VMEM((ROWS, CELLS), BF16),
        in_specs=[hbm] * 6,
        out_specs=pl.BlockSpec(memory_space=pltpu.VMEM),
        scratch_shapes=[
            pltpu.VMEM((DIN, ROWS), BF16),
            pltpu.VMEM((1, NZ), F32),
            pltpu.VMEM((NZ, DIN), F32),
            pltpu.VMEM((1, ROWS), F32),
            pltpu.VMEM((ROWS, CELLS), BF16),
            pltpu.VMEM((CELLS, WIDTH), BF16),
            pltpu.VMEM((WIDTH, CELLS), BF16),
            pltpu.VMEM((ROWS, CELLS), F32),
            pltpu.VMEM((DIN, ROWS), F32),
            pltpu.VMEM((NY * NC, DIN, ROWS), F32),
            pltpu.VMEM((NX * NC, DIN, ROWS), F32),
            pltpu.VMEM((NZ, RANK, ROWS), F32),
            pltpu.VMEM((NZ, RANK, ROWS), BF16),
            pltpu.VMEM((NZ * NC, EACH, RANK, ROWS), BF16),
            pltpu.VMEM((NX, EACH, NC, RANK, ROWS), BF16),
            pltpu.VMEM((NX * PAIR, RANK), BF16),
            pltpu.VMEM((RANK, NY * PAIR), BF16),
            pltpu.VMEM((EACH, NX, PAIR, NY * PAIR), BF16),
            pltpu.VMEM((NY, EACH, NC, RANK, ROWS), BF16),
            pltpu.VMEM((NY, EACH, NC, RANK, ROWS), BF16),
            pltpu.VMEM((NC, EACH, RANK, ROWS), BF16),
            pltpu.VMEM((NZ, RANK, ROWS), BF16),
            pltpu.SemaphoreType.DMA((3, 4)),
            pltpu.SemaphoreType.DMA((7,)),
            pltpu.SemaphoreType.DMA((7,)),
        ],
        compiler_params=pltpu.CompilerParams(
            collective_id=0, has_side_effects=True, vmem_limit_bytes=32 * 1024 * 1024
        ),
    )(*operands)


def solution(mesh):
    in_specs = (P("runs", "cells"), P(None, "runs"), P("cells", None), P(), P(), P("runs"))
    out_specs = P("runs", "cells")
    return jax.shard_map(shards, mesh=mesh, in_specs=in_specs, out_specs=out_specs, check_vma=False)
```

time: 32.6 us -> 31.7 us (0.972)
  Pallas kernels: 31.6 us -> 30.8 us
    pallas_call x1, Pallas kernels: 31.6 us -> 30.8 us  [shards(): pl.pallas_call(kernel, out_shape=pltpu.VMEM((ROWS, CELLS), BF16), in_spec...]
where the time goes in v5:
time: 31.7 us; the launch traced here: 31.6 us
  Pallas kernels  30.8 us (97%)
  local copies, waits for them, and re-layouts  0.8 us (3%)
    pallas_call x1, Pallas kernels, shards(): pl.pallas_call(kernel, out_shape=pltpu.VMEM((ROWS, CELLS), BF16), in_spec...  30.8 us
    unnamed x1, local copies, waits for them, and re-layouts  0.8 us

profile of v5, /device:TPU:1, one launch (start us, length us, event | category | flops | bytes accessed | tf_op | source)
XLA Modules:
  0.0 31.6 jit_solution(17693944467922419810)
XLA Ops:
  0.0 30.8 %shard_map.64 = bf16[128,2048]{1,0:T(8,128)(2,1)S(1)} custom-call(bf16[8,128]{1,0:T(8,128)(2,1)} %x_hbm.1, f32[1,8]{1,0:T(1,128)} %bitcast.2, f32[8,8]{1,0:T(8,128)} %len_hbm.1, f32[1,128]{1,0:T(1,128)} %bitcast.3, bf16[128,2048]{1,0:T(8,128)(2,1)} %maps_hbm.1, bf16[2048,256]{1,0:T(8,128)(2,1)} %basis_hbm.1), custom_call_target="tpu_custom_call" | custom-call | tf_op jit(solution)/shard_map/pallas_call | solution.py:296
  30.8 0.8 %copy.8 = bf16[128,2048]{1,0:T(8,128)(2,1)} copy(bf16[128,2048]{1,0:T(8,128)(2,1)S(1)} %shard_map.64) | data formatting | bytes 1048576

commit v6 on v5

--- a/solution.py
+++ b/solution.py
@@ -20,7 +20,8 @@
 LOADS = 2
 STEP = CELLS // LOADS
 FAR = (4, 3, 5, 2, 6, 1, 7)
-ROW, COL, PART, PROJ, SUM, LAT0, LAT1 = range(7)
+TURN = (0, 1, 2, 7, 3, 6, 5, 4)
+ROW, COL, PART, PART_LATE, PROJ, SUM, LAT0, LAT1 = range(8)
 
 
 def split3(value):
@@ -40,7 +41,7 @@
 def kernel(
     x_hbm, amp_hbm, len_hbm, noise_hbm, maps_hbm, basis_hbm, out_ref,
     x_ref, amp_ref, len_ref, noise_ref, maps, basis, basis_t, base, mine, rows_x, cols_x,
-    part_wide, part, part_in, proj, left, side, tile, sums, sums_in, lat_src, latent,
+    part, part_in, proj, left, side, tile, sums, sums_in, lat_src, latent,
     load_sem, send_sem, recv_sem,
 ):
     run = lax.axis_index("runs")
@@ -90,10 +91,10 @@
             for to in range(NC):
                 greet(at(0, 0, to, d))
 
-    def remote(phase, source, target, device):
+    def remote(phase, source, target, device, arrival=None):
         return pltpu.make_async_remote_copy(
             src_ref=source, dst_ref=target, send_sem=send_sem.at[phase],
-            recv_sem=recv_sem.at[phase], device_id=device, device_id_type=MESH,
+            recv_sem=recv_sem.at[phase if arrival is None else arrival], device_id=device, device_id_type=MESH,
         )
 
     def received(phase, target):
@@ -112,7 +113,6 @@
         now = pl.ds(c * STEP, STEP)
         total = total + jnp.dot(maps[:, now], basis[now, :], preferred_element_type=F32)
     turned = total.T.reshape(NZ, RANK, ROWS)
-    part_wide[...] = turned
     part[...] = turned.astype(BF16)
 
     @pl.when(late)
@@ -127,14 +127,13 @@
     def _():
         pl.semaphore_wait(barrier, OWNERS + NY + NX - 3)
 
-    for step in range(OWNERS):
-        plane = 3 - step
+    for plane in (2, 0, 3, 1):
 
         @pl.when(jnp.logical_or(core == 0, z != plane))
         def _():
-            slot = ((plane - z + NZ) % NZ) * NC + core
             source = part.at[pl.ds(plane * EACH, EACH)]
-            remote(PART, source, part_in.at[slot], at(0, 0, 1, plane - z)).start()
+            device = at(0, 0, 1, plane - z)
+            remote(PART, source, part_in.at[z * NC + core], device, PART + late.astype(jnp.int32)).start()
 
     for load in small:
         load.wait()
@@ -208,14 +207,25 @@
             cols_x[to] = rows_x[to]
         make_tile(0)
 
-        received(PART, part_in.at[pl.ds(0, NZ * NC - 1)])
+        part_in[z * NC + 1] = part[pl.ds(first, EACH)]
+        half = OWNERS * NC
+
+        def add(total, begin):
+            for k in range(begin, begin + half, NC):
+                total = [
+                    [total[slot][to] + part_in[k + to, slot].astype(F32) for to in range(NC)]
+                    for slot in range(EACH)
+                ]
+            return total
+
+        zero = [[jnp.zeros((RANK, ROWS), F32)] * NC] * EACH
+        received(PART, part_in.at[pl.ds(0, half - 1)])
+        own = add(zero, 0)
+        received(PART_LATE, part_in.at[pl.ds(half, half)])
+        own = add(own, half)
         for slot in range(EACH):
-            own = [part_in[0, slot].astype(F32), part_wide[first + slot]]
-            for d in range(1, NZ):
-                for to in range(NC):
-                    own[to] = own[to] + part_in[d * NC + to, slot].astype(F32)
-            for to in range(NC):
-                proj[0, slot, to] = own[to].astype(BF16)
+            for to in range(NC):
+                proj[0, slot, to] = own[slot][to].astype(BF16)
         for d in (2, 1, 3):
             remote(PROJ, proj.at[0], proj.at[d], at(0, d, 1, 0)).start()
         for slot in range(1, EACH):
@@ -229,17 +239,29 @@
                 values = values + jnp.dot(block, tile[slot, e, :, now], preferred_element_type=F32)
             return values
 
+        def look_up(values, index):
+            found = jnp.int32(values[0])
+            for k in range(1, len(values)):
+                found = jnp.where(index == k, values[k], found)
+            return found
+
+        place_y = look_up([TURN.index(k) for k in range(NY)], y)
+        turns = [look_up(TURN, step + (step >= place_y).astype(jnp.int32)) for step in range(NY - 1)]
         received(PROJ, proj.at[pl.ds(1, NX - 1)])
 
-        for step in range(NY - 1):
-            to_y = step + (step >= y).astype(jnp.int32)
+        for to_y in turns:
             row = (y - to_y + NY) % NY
             for slot in range(EACH):
                 values = product(row, slot)
                 for to in range(NC):
                     sums[row, slot, to] = values[:, to * ROWS:(to + 1) * ROWS].astype(BF16)
-            remote(SUM, sums.at[row], sums_in.at[row], at(to_y - y, 0, 1, 0)).start()
+                remote(SUM, sums.at[row, slot], sums_in.at[row, slot], at(to_y - y, 0, 1, 0)).start()
         own = [product(0, slot) for slot in range(EACH)]
+        left_here(ROW, rows_x.at[pl.ds(0, NY - 1)])
+        left_here(COL, cols_x.at[pl.ds(0, NX - 1)])
+        left_here(PART, part.at[pl.ds(0, NZ - EACH)])
+        left_here(PROJ, proj.at[pl.ds(1, NX - 1)])
+        left_here(SUM, sums.at[pl.ds(0, NY - 1)])
         received(SUM, sums_in.at[pl.ds(1, NY - 1)])
         for slot in range(EACH):
             for to in range(NC):
@@ -256,13 +278,6 @@
         for slot in range(EACH):
             latent[first + slot] = lat_src[1, slot]
 
-        left_here(ROW, rows_x.at[pl.ds(0, NY - 1)])
-        left_here(COL, cols_x.at[pl.ds(0, NX - 1)])
-        left_here(PART, part.at[pl.ds(0, NZ - EACH)])
-        left_here(PROJ, proj.at[pl.ds(1, NX - 1)])
-        left_here(SUM, sums.at[pl.ds(0, NY - 1)])
-        left_here(LAT0, part_in.at[pl.ds(0, NZ)])
-        left_here(LAT1, part_in.at[pl.ds(0, NZ - 1)])
         received(LAT1, latent.at[pl.ds(0, NZ - EACH)])
 
     @pl.when(jnp.logical_not(owner))
@@ -287,6 +302,11 @@
         now = pl.ds(c * STEP, STEP)
         expand = jnp.dot(mixed, basis_t[:, now], preferred_element_type=F32)
         out_ref[:, now] = (expand + base[:, now]).astype(BF16)
+
+    @pl.when(owner)
+    def _():
+        left_here(LAT0, part_in.at[pl.ds(0, NZ)])
+        left_here(LAT1, part_in.at[pl.ds(0, NZ - 1)])
 
 
 def shards(maps, run_inputs, basis, amplitude, length, noise):
@@ -310,7 +330,6 @@
             pltpu.VMEM((DIN, ROWS), F32),
             pltpu.VMEM((NY * NC, DIN, ROWS), F32),
             pltpu.VMEM((NX * NC, DIN, ROWS), F32),
-            pltpu.VMEM((NZ, RANK, ROWS), F32),
             pltpu.VMEM((NZ, RANK, ROWS), BF16),
             pltpu.VMEM((NZ * NC, EACH, RANK, ROWS), BF16),
             pltpu.VMEM((NX, EACH, NC, RANK, ROWS), BF16),
@@ -322,8 +341,8 @@
             pltpu.VMEM((NC, EACH, RANK, ROWS), BF16),
             pltpu.VMEM((NZ, RANK, ROWS), BF16),
             pltpu.SemaphoreType.DMA((3, 4)),
-            pltpu.SemaphoreType.DMA((7,)),
-            pltpu.SemaphoreType.DMA((7,)),
+            pltpu.SemaphoreType.DMA((8,)),
+            pltpu.SemaphoreType.DMA((8,)),
         ],
         compiler_params=pltpu.CompilerParams(
             collective_id=0, has_side_effects=True, vmem_limit_bytes=32 * 1024 * 1024

time: 31.7 us -> 31.8 us (level)
  no operation moved by 1% of the time
where the time goes in v6:
time: 31.8 us; the launch traced here: 31.7 us
  Pallas kernels  30.8 us (97%)
  local copies, waits for them, and re-layouts  0.8 us (3%)
    pallas_call x1, Pallas kernels, shards(): pl.pallas_call(kernel, out_shape=pltpu.VMEM((ROWS, CELLS), BF16), in_spec...  30.8 us
    unnamed x1, local copies, waits for them, and re-layouts  0.8 us

profile of v6, /device:TPU:1, one launch (start us, length us, event | category | flops | bytes accessed | tf_op | source)
XLA Modules:
  0.0 31.7 jit_solution(13566278210797515262)
XLA Ops:
  0.0 30.8 %shard_map.64 = bf16[128,2048]{1,0:T(8,128)(2,1)S(1)} custom-call(bf16[8,128]{1,0:T(8,128)(2,1)} %x_hbm.1, f32[1,8]{1,0:T(1,128)} %bitcast.2, f32[8,8]{1,0:T(8,128)} %len_hbm.1, f32[1,128]{1,0:T(1,128)} %bitcast.3, bf16[128,2048]{1,0:T(8,128)(2,1)} %maps_hbm.1, bf16[2048,256]{1,0:T(8,128)(2,1)} %basis_hbm.1), custom_call_target="tpu_custom_call" | custom-call | tf_op jit(solution)/shard_map/pallas_call | solution.py:316
  30.9 0.8 %copy.8 = bf16[128,2048]{1,0:T(8,128)(2,1)} copy(bf16[128,2048]{1,0:T(8,128)(2,1)S(1)} %shard_map.64) | data formatting | bytes 1048576

commit v7 on v6

--- a/solution.py
+++ b/solution.py
@@ -297,7 +297,7 @@
         def _():
             received(LAT1, latent)
 
-    mixed = latent[...].reshape(WIDTH, ROWS).astype(F32).T.astype(BF16)
+    mixed = latent[...].reshape(WIDTH, ROWS).T
     for c in range(LOADS):
         now = pl.ds(c * STEP, STEP)
         expand = jnp.dot(mixed, basis_t[:, now], preferred_element_type=F32)

time: 31.8 us -> 31.8 us (level)
  no operation moved by 1% of the time
where the time goes in v7:
time: 31.8 us; the launch traced here: 31.6 us
  Pallas kernels  30.8 us (97%)
  local copies, waits for them, and re-layouts  0.8 us (3%)
    pallas_call x1, Pallas kernels, shards(): pl.pallas_call(kernel, out_shape=pltpu.VMEM((ROWS, CELLS), BF16), in_spec...  30.8 us
    unnamed x1, local copies, waits for them, and re-layouts  0.8 us

profile of v7, /device:TPU:1, one launch (start us, length us, event | category | flops | bytes accessed | tf_op | source)
XLA Modules:
  0.0 31.6 jit_solution(16010758317841187998)
XLA Ops:
  0.0 30.8 %shard_map.64 = bf16[128,2048]{1,0:T(8,128)(2,1)S(1)} custom-call(bf16[8,128]{1,0:T(8,128)(2,1)} %x_hbm.1, f32[1,8]{1,0:T(1,128)} %bitcast.2, f32[8,8]{1,0:T(8,128)} %len_hbm.1, f32[1,128]{1,0:T(1,128)} %bitcast.3, bf16[128,2048]{1,0:T(8,128)(2,1)} %maps_hbm.1, bf16[2048,256]{1,0:T(8,128)(2,1)} %basis_hbm.1), custom_call_target="tpu_custom_call" | custom-call | tf_op jit(solution)/shard_map/pallas_call | solution.py:316
  30.8 0.8 %copy.8 = bf16[128,2048]{1,0:T(8,128)(2,1)} copy(bf16[128,2048]{1,0:T(8,128)(2,1)S(1)} %shard_map.64) | data formatting | bytes 1048576
